TPU v7x, 32 devices: a whole 2x2x4 slice. The times are simulated.
32 devices in a mesh: row: 4 (over y, x), col: 8 (over z, core).
Axes of the slice: x: 2, y: 2, z: 4, core: 2. Of those that a mesh axis runs over, the one named last changes fastest.
Arguments:
- front: float32 [16, 4, 128, 8, 8, 128], P(None, 'row', None, None, 'col'), as said below
- block_slots: int32 [64], replicated, may hold values from 0 to 63, as said below
- rows_first: int32 [39], replicated, may hold values from 4 to 63, as said below
- rows_second: int32 [49], replicated, may hold values from 8 to 63, as said below
Outputs:
- factored: float32 [16, 4, 128, 8, 8, 128], P(None, 'row', None, None, 'col')
Inputs may be any that keep to these rules, and one draw needn't show every extreme that they name: front is symmetric, and its square on the slots of blocks 0 to 7 is positive definite. `block_slots`: each slot appears once. `rows_second`: 49 distinct block numbers in increasing order; 8 and 63 are always among them. `rows_first`: 4, 5, 6, 7, then 39 - 4 distinct block numbers in increasing order, all of them in rows_second, 63 always among them.
All inputs are finite; a program needn't handle non-finite values.
Results may differ from a plain program's by a relative error of at most 0.00028.
Values sent between devices are 32-bit elements; how exact they have to be, the bound alone decides.
No kernel may reach another device: no remote copies, remote signals or barrier semaphores. Data moves between devices by JAX's collectives and lax.ppermute only.
A program may use at most 128 MiB of HBM per device.

v0:
```python
import functools

import jax
import jax.numpy as jnp
from jax import lax
from jax.experimental import pallas as pl
from jax.experimental.pallas import tpu as pltpu
from jax.sharding import PartitionSpec as P

BS = 128
PB = 4
NC = 2 * PB
STEP = 4
ALMOST_ALL = 63 * 2**20
HIGHEST = lax.Precision.HIGHEST
HBM = pl.BlockSpec(memory_space=pltpu.HBM)
VMEM = pl.BlockSpec(memory_space=pltpu.VMEM)
SMEM = pl.BlockSpec(memory_space=pltpu.SMEM)


def lane_copy(tile, lane):
    return jnp.broadcast_to(tile[:, lane : lane + 1], tile.shape)


def row_copy(tile, row):
    return jnp.broadcast_to(tile[row : row + 1, :], tile.shape)


def factor_block(block):
    tiles = BS // 8
    sub = lax.broadcasted_iota(jnp.int32, (8, BS), 0)
    lanes = lax.broadcasted_iota(jnp.int32, (8, BS), 1)
    left = [block[8 * i : 8 * i + 8, :] for i in range(tiles)]
    right = [jnp.where(lanes == sub + 8 * i, 1.0, 0.0).astype(jnp.float32) for i in range(tiles)]
    upper = []
    inverse = []
    for j in range(0, BS, STEP):
        g, o = divmod(j, 8)
        if o == 0:
            upper_tile = jnp.zeros((8, BS), jnp.float32)
            inverse_tile = jnp.zeros((8, BS), jnp.float32)
        rows = [row_copy(left[g], o + s) for s in range(STEP)]
        extra = [row_copy(right[g], o + s) for s in range(STEP)]
        first = g if o + STEP < 8 else g + 1
        cols = {i: [lane_copy(left[i], j + s) for s in range(STEP)] for i in range(first, tiles)}
        pivot = [[lane_copy(rows[s], j + t) if t >= s else None for t in range(STEP)] for s in range(STEP)]
        ratio = [[None] * STEP for _ in range(STEP)]
        recip = []
        for s in range(STEP):
            inv = 1.0 / pivot[s][s]
            recip.append(inv)
            for t in range(s + 1, STEP):
                ratio[s][t] = pivot[s][t] * inv
            for t in range(s + 1, STEP):
                for u in range(t, STEP):
                    pivot[t][u] = pivot[t][u] - ratio[s][t] * pivot[s][u]
                rows[t] = rows[t] - ratio[s][t] * rows[s]
                extra[t] = extra[t] - ratio[s][t] * extra[s]
        for s in range(STEP):
            scale = lax.rsqrt(pivot[s][s])
            scale = scale * (1.5 - 0.5 * pivot[s][s] * scale * scale)
            here = sub == o + s
            upper_tile = jnp.where(here, rows[s] * scale, upper_tile)
            inverse_tile = jnp.where(here, extra[s] * scale, inverse_tile)
        if o + STEP == 8:
            upper.append(jnp.where(lanes >= sub + 8 * g, upper_tile, 0.0))
            inverse.append(jnp.where(lanes <= sub + 8 * g, inverse_tile, 0.0))
        for s in reversed(range(STEP)):
            rows[s] = rows[s] * recip[s]
            extra[s] = extra[s] * recip[s]
            for t in range(s + 1, STEP):
                rows[s] = rows[s] - ratio[s][t] * rows[t]
                extra[s] = extra[s] - ratio[s][t] * extra[t]
        for i in range(first, tiles):
            less = cols[i][0] * rows[0]
            less_extra = cols[i][0] * extra[0]
            for s in range(1, STEP):
                less = less + cols[i][s] * rows[s]
                less_extra = less_extra + cols[i][s] * extra[s]
            if i == g:
                below = sub >= o + STEP
                left[i] = jnp.where(below, left[i] - less, left[i])
                right[i] = jnp.where(below, right[i] - less_extra, right[i])
            else:
                left[i] = left[i] - less
                right[i] = right[i] - less_extra
    return jnp.concatenate(upper, axis=0), jnp.concatenate(inverse, axis=0)


def lower_index(i, j):
    return i * (i + 1) // 2 + j


def dot_nt(a, b):
    return lax.dot_general(a, b, (((1,), (1,)), ((), ())), precision=HIGHEST, preferred_element_type=jnp.float32)


def dot_nn(a, b):
    return lax.dot_general(a, b, (((1,), (0,)), ((), ())), precision=HIGHEST, preferred_element_type=jnp.float32)


def split(x):
    high = x.astype(jnp.bfloat16)
    return high, (x - high.astype(jnp.float32)).astype(jnp.bfloat16)


def place(count, core, block):
    half = count // 2
    return (block // half) == core, block % half


def start_kernel(slots, first, second, front_ref, flags, token, panel, keep, send, zero, blocks, columns, sems, out_sems):
    row_blocks, _, col_blocks = front_ref.shape[:3]
    grid_rows, grid_cols = 4, 8
    own_row = lax.axis_index("row")
    own_col = lax.axis_index("col")
    core = own_col % 2
    slot = [slots[i] for i in range(NC)]
    count = NC * (NC + 1) // 2
    half = count // 2
    moves = []
    fills = []

    def move(condition, source, middle, targets):
        index = len(moves)

        @pl.when(condition)
        def _():
            pltpu.make_async_copy(source, middle, sems.at[index]).start()

        moves.append((condition, middle, targets, index))

    always = core >= 0
    group = zero.shape[0]
    for c in range(NC):
        owned = slot[c] % grid_cols == own_col
        for a in range(0, row_blocks, group):
            fills.append((jnp.logical_not(owned), zero, panel.at[c, a : a + group], len(moves)))
        move(owned, front_ref.at[:, :, slot[c] // grid_cols], columns.at[c], ((panel.at[c], always),))
    for i in range(NC):
        for j in range(i + 1):
            block = lower_index(i, j)
            a = slot[i] // grid_rows
            b = slot[j] // grid_cols
            owned = jnp.logical_and(slot[i] % grid_rows == own_row, slot[j] % grid_cols == own_col)
            stay = core == block // half
            targets = ((keep.at[block % half], stay), (send.at[block % half], jnp.logical_not(stay)))
            for target, chosen in targets:
                fills.append((jnp.logical_and(chosen, jnp.logical_not(owned)), zero.at[0], target, len(moves)))
            move(owned, front_ref.at[a, :, b], blocks.at[block], targets)

    zero[...] = jnp.zeros_like(zero)
    for condition, source, target, index in fills:
        @pl.when(condition)
        def _(source=source, target=target, index=index):
            pltpu.make_async_copy(source, target, out_sems.at[index]).start()

    for a in range(row_blocks):
        for f in range(8):
            flags[a, f] = jnp.int32(-1 if f in (2, 5) else 0)
    for c in range(NC):
        @pl.when(slot[c] % grid_rows == own_row)
        def _(c=c):
            flags[slot[c] // grid_rows, 2] = jnp.int32(c)

        @pl.when(slot[c] % grid_cols == own_col)
        def _(c=c):
            flags[slot[c] // grid_cols, 5] = jnp.int32(c)

    for listed, f in ((first, 0), (second, 1)):
        @pl.loop(0, listed.shape[0])
        def _(i, listed=listed, f=f):
            s = slots[listed[i]]

            @pl.when(s % grid_rows == own_row)
            def _():
                flags[s // grid_rows, f] = jnp.int32(1)

            @pl.when(s % grid_cols == own_col)
            def _():
                flags[s // grid_cols, 3 + f] = jnp.int32(1)

    token[0] = jnp.int32(0)
    for condition, middle, targets, index in moves:
        @pl.when(condition)
        def _(middle=middle, targets=targets, index=index):
            pltpu.make_async_copy(middle, middle, sems.at[index]).wait()
            for target, chosen in targets:
                @pl.when(chosen)
                def _(target=target):
                    pltpu.make_async_copy(middle, target, out_sems.at[index]).start()
    for condition, middle, targets, index in moves:
        pltpu.make_async_copy(middle, middle, out_sems.at[index]).wait()


TOKEN = jax.ShapeDtypeStruct((1,), jnp.int32)


def start(front, block_slots, rows_first, rows_second):
    row_blocks, col_blocks = front.shape[0], front.shape[3]
    count = NC * (NC + 1) // 2
    f32 = lambda *shape: jax.ShapeDtypeStruct(shape, jnp.float32)
    flags, token, panel, keep, send = pl.pallas_call(
        start_kernel,
        out_shape=(
            jax.ShapeDtypeStruct((row_blocks, 8), jnp.int32),
            TOKEN,
            f32(NC, row_blocks, BS, 1, BS),
            f32(count // 2, BS, 1, BS),
            f32(count // 2, BS, 1, BS),
        ),
        in_specs=[SMEM, SMEM, SMEM, HBM],
        out_specs=(SMEM, SMEM) + (HBM,) * 3,
        scratch_shapes=[
            pltpu.VMEM((row_blocks // 4, BS, 1, BS), jnp.float32),
            pltpu.VMEM((count, BS, 1, BS), jnp.float32),
            pltpu.VMEM((NC, row_blocks, BS, 1, BS), jnp.float32),
            pltpu.SemaphoreType.DMA((count + NC,)),
            pltpu.SemaphoreType.DMA((count + NC,)),
        ],
        compiler_params=pltpu.CompilerParams(vmem_limit_bytes=ALMOST_ALL),
        name="start",
    )(block_slots, rows_first, rows_second, front.reshape(row_blocks, BS, col_blocks, 1, BS))
    return flags, token, panel.reshape(NC, row_blocks, BS, BS), keep.reshape(-1, BS), send.reshape(-1, BS)


def lines_kernel(slots, after, wide_ref, one, two, token, zero, lines, sems, out_sems):
    own_row = lax.axis_index("row")
    owned = [slots[c] % 4 == own_row for c in range(NC)]
    targets = [(one if c < PB else two).at[c % PB] for c in range(NC)]
    for c in range(NC):
        @pl.when(owned[c])
        def _(c=c):
            pltpu.make_async_copy(wide_ref.at[slots[c] // 4], lines.at[c], sems.at[c]).start()
    zero[...] = jnp.zeros_like(zero)
    for c in range(NC):
        @pl.when(jnp.logical_not(owned[c]))
        def _(c=c):
            pltpu.make_async_copy(zero, targets[c], out_sems.at[c]).start()
    for c in range(NC):
        @pl.when(owned[c])
        def _(c=c):
            pltpu.make_async_copy(lines.at[c], lines.at[c], sems.at[c]).wait()
            pltpu.make_async_copy(lines.at[c], targets[c], out_sems.at[c]).start()
    token[0] = jnp.int32(0)
    for c in range(NC):
        pltpu.make_async_copy(zero, targets[c], out_sems.at[c]).wait()


def lines(front, block_slots, after):
    row_blocks, col_blocks = front.shape[0], front.shape[3]
    part = jax.ShapeDtypeStruct((PB, BS, col_blocks, BS), jnp.float32)
    return pl.pallas_call(
        lines_kernel,
        out_shape=(part, part, TOKEN),
        in_specs=[SMEM, SMEM, HBM],
        out_specs=(HBM, HBM, SMEM),
        scratch_shapes=[
            pltpu.VMEM((BS, col_blocks, BS), jnp.float32),
            pltpu.VMEM((NC, BS, col_blocks, BS), jnp.float32),
            pltpu.SemaphoreType.DMA((NC,)),
            pltpu.SemaphoreType.DMA((NC,)),
        ],
        name="lines",
    )(block_slots, after, local_blocks(front))


def add_kernel(after, a, b, c, d, first, second, token):
    first[...] = a[...] + b[...]
    second[...] = c[...] + d[...]

    @pl.when(pl.program_id(0) == 0)
    def _():
        token[0] = jnp.int32(0)


def add_pairs(a, b, c, d, after):
    block = pl.BlockSpec((1,) + a.shape[1:], lambda i: (i,) + (0,) * (a.ndim - 1))
    return pl.pallas_call(
        add_kernel,
        out_shape=(jax.ShapeDtypeStruct(a.shape, a.dtype),) * 2 + (TOKEN,),
        grid=(a.shape[0],),
        in_specs=[SMEM] + [block] * 4,
        out_specs=(block, block, SMEM),
        name="add_pairs",
    )(after, a, b, c, d)


def permute(value, flip):
    pairs = []
    for p in range(4):
        for q in range(8):
            to_p, to_q = flip(p, q)
            if 0 <= to_q < 8:
                pairs.append((p * 8 + q, to_p * 8 + to_q))
    return lax.ppermute(value, ("row", "col"), pairs)


def swap_core(value):
    return permute(value, lambda p, q: (p, q ^ 1))


def place(axis):
    return lax.axis_index("row") if axis == "row" else lax.axis_index("col") // 2


def spread_kernel(axis, count, *refs):
    total = refs[-1]
    outs = refs[count:-1]
    value = refs[0][...]
    for ref in refs[1:count]:
        value = value + ref[...]
    total[...] = value
    own = place(axis)
    for d in range(4):
        outs[d][...] = total[own ^ d]


def spread(axis, terms):
    rows = terms[0].shape[0] // 4
    shape = (4, rows, BS)
    return pl.pallas_call(
        functools.partial(spread_kernel, axis, len(terms)),
        out_shape=(jax.ShapeDtypeStruct((rows, BS), jnp.float32),) * 4,
        in_specs=[VMEM] * len(terms),
        out_specs=(VMEM,) * 4,
        scratch_shapes=[pltpu.VMEM(shape, jnp.float32)],
        name="spread",
    )(*[term.reshape(shape) for term in terms])


def collect_kernel(axis, own, one, two, three, out):
    at = place(axis)
    for d, source in enumerate((own, one, two, three)):
        out[at ^ d] = source[...]


def collect(axis, own, others):
    rows = own.shape[0]
    out = pl.pallas_call(
        functools.partial(collect_kernel, axis),
        out_shape=jax.ShapeDtypeStruct((4, rows, BS), jnp.float32),
        in_specs=[VMEM] * 4,
        out_specs=VMEM,
        name="collect",
    )(own, *others)
    return out.reshape(4 * rows, BS)


def join_kernel(own, other, first, second, token):
    core = lax.axis_index("col") % 2
    one = first.shape[0]
    half = own.shape[0]
    for which, low, high in ((0, own, other), (1, other, own)):
        @pl.when(core == which)
        def _(low=low, high=high):
            first[...] = low[:one]
            second[: half - one] = low[one:]
            second[half - one :] = high[...]
    token[0] = jnp.int32(0)


def join(own):
    other = swap_core(own)
    one = PB * (PB + 1) // 2
    count = NC * (NC + 1) // 2
    block = lambda n: jax.ShapeDtypeStruct((n, BS, BS), jnp.float32)
    return pl.pallas_call(
        join_kernel,
        out_shape=(block(one), block(count - one), TOKEN),
        in_specs=[VMEM] * 2,
        out_specs=(VMEM, VMEM, SMEM),
        name="join",
    )(own.reshape(-1, BS, BS), other.reshape(-1, BS, BS))


def across(axis, parts):
    if axis == "row":
        return [permute(parts[d - 1], lambda p, q, d=d: (p ^ d, q)) for d in range(1, 4)]
    return [permute(parts[d - 1], lambda p, q, d=d: (p, q ^ (2 * d))) for d in range(1, 4)]


def sum_square(keep, send):
    own, *parts = spread("row", [keep, swap_core(send)])
    own, *parts = spread("col", [own] + across("row", parts))
    got = across("col", parts)
    value = own + got[0] + got[1] + got[2]
    for axis in ("col", "row"):
        value = collect(axis, value, across(axis, [value] * 3))
    return join(value)


def piece_kernel(n, diag, *rest):
    lowers = rest[:n]
    inverses = rest[n : 2 * n]
    lower_out, inverse_out, token = rest[-3:]
    token[0] = jnp.int32(0)

    def row(i):
        return jnp.concatenate([lowers[j][(i - j) * BS : (i - j + 1) * BS, :] for j in range(n)], axis=1)

    column = []
    for i in range(n, PB):
        value = diag[lower_index(i, n)]
        if n:
            value = value - dot_nt(row(i), row(n))
        column.append(value)
    upper, inverse = factor_block(column[0])
    lower_out[0:BS, :] = upper.T
    if n + 1 < PB:
        lower_out[BS:, :] = dot_nt(jnp.concatenate(column[1:], axis=0), inverse)
    inverse_out[:, n * BS :] = inverse
    if n:
        before = jnp.concatenate(
            [
                jnp.concatenate([inverses[j][...], jnp.zeros((BS, (n - 1 - j) * BS), jnp.float32)], axis=1)
                if j + 1 < n
                else inverses[j][...]
                for j in range(n)
            ],
            axis=0,
        )
        inverse_out[:, : n * BS] = -dot_nn(inverse, dot_nn(row(n), before))


def piece(n, diag, lowers, inverses, after):
    return pl.pallas_call(
        functools.partial(piece_kernel, n),
        out_shape=(
            jax.ShapeDtypeStruct(((PB - n) * BS, BS), jnp.float32),
            jax.ShapeDtypeStruct((BS, (n + 1) * BS), jnp.float32),
            TOKEN,
        ),
        in_specs=[VMEM] * (1 + 2 * n) + [SMEM] * len(after),
        out_specs=(VMEM, VMEM, SMEM),
        compiler_params=pltpu.CompilerParams(vmem_limit_bytes=32 * 2**20),
        cost_estimate=pl.CostEstimate(flops=10**8, bytes_accessed=10**5, transcendentals=0),
        name="factor_piece",
    )(diag, *lowers, *inverses, *after)


def inverse_rows(inverses):
    rows = []
    for j in range(PB):
        if j + 1 < PB:
            rows.append(jnp.concatenate([inverses[j][...], jnp.zeros((BS, (PB - 1 - j) * BS), jnp.float32)], axis=1))
        else:
            rows.append(inverses[j][...])
    return jnp.concatenate(rows, axis=0)


def between_kernel(diag, *rest):
    inverses = rest[:PB]
    cross_out, rest_out = rest[-2:]
    inverse = inverse_rows(inverses)
    one = PB * (PB + 1) // 2
    left = [
        jnp.concatenate([diag[lower_index(i, j) - one] for j in range(PB)], axis=1) for i in range(PB, NC)
    ]
    cross = dot_nt(jnp.concatenate(left, axis=0), inverse)
    cross_out[...] = cross
    for i in range(PB):
        here = cross[i * BS : (i + 1) * BS, :]
        product = dot_nt(here, cross[: (i + 1) * BS, :])
        for j in range(i + 1):
            block = diag[lower_index(i + PB, j + PB) - one]
            rest_out[lower_index(i, j)] = block - product[:, j * BS : (j + 1) * BS]


def between(diag, inverses, after):
    return pl.pallas_call(
        between_kernel,
        out_shape=(
            jax.ShapeDtypeStruct((PB * BS, PB * BS), jnp.float32),
            jax.ShapeDtypeStruct((PB * (PB + 1) // 2, BS, BS), jnp.float32),
        ),
        in_specs=[VMEM] * (1 + PB) + [SMEM] * len(after),
        out_specs=(VMEM, VMEM),
        compiler_params=pltpu.CompilerParams(vmem_limit_bytes=32 * 2**20),
        cost_estimate=pl.CostEstimate(flops=10**8, bytes_accessed=10**5, transcendentals=0),
        name="between",
    )(diag, *inverses, *after)


def finish_kernel(*refs):
    first = inverse_rows(refs[:PB])
    second = inverse_rows(refs[PB : 2 * PB])
    cross = refs[2 * PB][...]
    lowers = refs[2 * PB + 1 : 4 * PB + 1]
    lower_out, high_out, low_out = refs[-3:]
    size = PB * BS
    lower_out[...] = jnp.zeros_like(lower_out)
    for j in range(PB):
        for half in range(2):
            rows = slice(half * size + j * BS, (half + 1) * size)
            lower_out[rows, j * BS : (j + 1) * BS] = lowers[half * PB + j][...]
    high_out[:size, size:] = jnp.zeros((size, size), jnp.bfloat16)
    low_out[:size, size:] = jnp.zeros((size, size), jnp.bfloat16)
    corner = -dot_nn(second, dot_nn(cross, first))
    for value, rows, cols in (
        (first, slice(0, size), slice(0, size)),
        (corner, slice(size, 2 * size), slice(0, size)),
        (second, slice(size, 2 * size), slice(size, 2 * size)),
    ):
        high, low = split(value)
        high_out[rows, cols] = high
        low_out[rows, cols] = low


def finish(first, second, cross, lowers):
    size = NC * BS
    return pl.pallas_call(
        finish_kernel,
        out_shape=(jax.ShapeDtypeStruct((size, size // 2), jnp.float32),)
        + (jax.ShapeDtypeStruct((size, size), jnp.bfloat16),) * 2,
        in_specs=[VMEM] * (4 * PB + 1),
        out_specs=(VMEM,) * 3,
        compiler_params=pltpu.CompilerParams(vmem_limit_bytes=32 * 2**20),
        cost_estimate=pl.CostEstimate(flops=10**8, bytes_accessed=10**5, transcendentals=0),
        name="finish",
    )(*first, *second, cross, *lowers)


def three(dot, a_high, a_low, b_high, b_low):
    kwargs = dict(preferred_element_type=jnp.float32)
    return dot(a_high, b_high, **kwargs) + (dot(a_high, b_low, **kwargs) + dot(a_low, b_high, **kwargs))


def nt(a, b, **kwargs):
    return lax.dot_general(a, b, (((1,), (1,)), ((), ())), **kwargs)


def nn(a, b, **kwargs):
    return lax.dot_general(a, b, (((1,), (0,)), ((), ())), **kwargs)


def masked(tiles, axis, first, second):
    low_part = jnp.concatenate(tiles[:PB], axis=axis)
    high_part = jnp.concatenate(tiles[PB:], axis=axis)
    zero = jnp.zeros_like(low_part)
    return jnp.concatenate([jnp.where(first, low_part, zero), jnp.where(second, high_part, zero)], axis=axis)


def columns_kernel(flags, one, one_more, two, two_more, high_ref, low_ref, col_high, col_low, raw_high, raw_low):
    size = NC * BS
    half = PB * BS
    width = 2 * BS
    col_blocks = one.shape[2]
    for b in range(col_blocks):
        at = slice(b * BS, (b + 1) * BS)
        tiles = [one[c, :, b, :] + one_more[c, :, b, :] for c in range(PB)]
        tiles += [two[c, :, b, :] + two_more[c, :, b, :] for c in range(PB)]
        raw = masked(tiles, 0, flags[b, 3] != 0, flags[b, 4] != 0)
        high, low = split(raw)
        raw_high[:, at] = high
        raw_low[:, at] = low
    for m in range(0, size, width):
        deep = m + width
        value = three(nn, high_ref[m:deep, :deep], low_ref[m:deep, :deep], raw_high[:deep, :], raw_low[:deep, :])
        if m >= half:
            value = jnp.concatenate(
                [jnp.where(flags[b, 4] != 0, value[:, b * BS : (b + 1) * BS], 0.0) for b in range(col_blocks)],
                axis=1,
            )
        high, low = split(value)
        col_high[m:deep, :] = high
        col_low[m:deep, :] = low


def solve_columns(flags, one, one_more, two, two_more, high, low):
    size = NC * BS
    shape = (size, one.shape[2] * BS)
    return pl.pallas_call(
        columns_kernel,
        out_shape=(jax.ShapeDtypeStruct(shape, jnp.bfloat16),) * 2,
        in_specs=[SMEM] + [VMEM] * 6,
        out_specs=(VMEM, VMEM),
        scratch_shapes=[pltpu.VMEM(shape, jnp.bfloat16), pltpu.VMEM(shape, jnp.bfloat16)],
        compiler_params=pltpu.CompilerParams(vmem_limit_bytes=48 * 2**20),
        cost_estimate=pl.CostEstimate(flops=10**9, bytes_accessed=10**6, transcendentals=0),
        name="solve_columns",
    )(flags, one, one_more, two, two_more, high, low)


def update_kernel(flags, front_ref, rows_ref, lower_ref, high_ref, low_ref, col_high, col_low, out_ref,
                  solved, sol_high, sol_low):
    size = NC * BS
    half = PB * BS
    width = 2 * BS
    step = pl.program_id(0)
    col_blocks = front_ref.shape[1]
    for k in range(2):
        a = step * 2 + k
        raw = masked([rows_ref[c, k] for c in range(NC)], 1, flags[a, 0] != 0, flags[a, 1] != 0)
        high, low = split(raw)
        sol_high[k * BS : (k + 1) * BS, :] = high
        sol_low[k * BS : (k + 1) * BS, :] = low
    for m in range(0, size, width):
        deep = m + width
        value = three(nt, sol_high[:, :deep], sol_low[:, :deep], high_ref[m:deep, :deep], low_ref[m:deep, :deep])
        if m >= half:
            value = jnp.concatenate(
                [
                    jnp.where(flags[step * 2 + k, 1] != 0, value[k * BS : (k + 1) * BS, :], 0.0)
                    for k in range(2)
                ],
                axis=0,
            )
        solved[:, m:deep] = value
    high, low = split(solved[...])
    sol_high[...] = high
    sol_low[...] = low
    for b in range(0, col_blocks, 2):
        at = slice(b * BS, (b + 2) * BS)
        value = three(nn, sol_high[...], sol_low[...], col_high[:, at], col_low[:, at])
        for s in range(2):
            out_ref[:, b + s, :] = front_ref[:, b + s, :] - value[:, s * BS : (s + 1) * BS]
    for b in range(col_blocks):
        j = flags[b, 5]

        @pl.when(j >= 0)
        def _(b=b, j=j):
            at = pl.ds(pl.multiple_of(j * BS, BS), BS)
            for k in range(2):
                a = step * 2 + k
                rows = slice(k * BS, (k + 1) * BS)
                listed = jnp.where(j < PB, flags[a, 0], flags[a, 1])
                own = flags[a, 2]

                @pl.when(listed != 0)
                def _():
                    out_ref[rows, b, :] = solved[rows, at]

                @pl.when(jnp.logical_and(own >= 0, own // PB == j // PB))
                def _():
                    source = pl.ds(pl.multiple_of(own * BS, BS), BS)
                    inside = pl.ds(pl.multiple_of(j % PB * BS, BS), BS)
                    out_ref[rows, b, :] = lower_ref[source, inside]


def update_front(flags, front, rows, lower, high, low, col_high, col_low):
    row_blocks, _, col_blocks = front.shape[:3]
    size = NC * BS
    block = pl.BlockSpec((2 * BS, col_blocks, BS), lambda i: (i, 0, 0))
    return pl.pallas_call(
        update_kernel,
        out_shape=jax.ShapeDtypeStruct((row_blocks * BS, col_blocks, BS), jnp.float32),
        grid=(row_blocks // 2,),
        in_specs=[SMEM, block, pl.BlockSpec((NC, 2, BS, BS), lambda i: (0, i, 0, 0))] + [VMEM] * 5,
        out_specs=block,
        scratch_shapes=[
            pltpu.VMEM((2 * BS, size), jnp.float32),
            pltpu.VMEM((2 * BS, size), jnp.bfloat16),
            pltpu.VMEM((2 * BS, size), jnp.bfloat16),
        ],
        compiler_params=pltpu.CompilerParams(vmem_limit_bytes=40 * 2**20),
        cost_estimate=pl.CostEstimate(flops=10**9, bytes_accessed=10**6, transcendentals=0),
        name="update_front",
    )(flags, front.reshape(row_blocks * BS, col_blocks, BS), rows, lower, high, low, col_high, col_low)


def block_flags(slots, listed_one, listed_two, diag_slots):
    one = jnp.any(slots[:, None] == listed_one[None, :], axis=1).astype(jnp.int32)
    two = jnp.any(slots[:, None] == listed_two[None, :], axis=1).astype(jnp.int32)
    order = jnp.arange(1, NC + 1, dtype=jnp.int32)
    where = jnp.sum(jnp.where(slots[:, None] == diag_slots[None, :], order[None, :], 0), axis=1) - 1
    return jnp.stack([one, two, where], axis=1)


def gather_summed(front, block_slots, rows_first, rows_second):
    grid_rows, grid_cols = lax.axis_size("row"), lax.axis_size("col")
    own_row, own_col = lax.axis_index("row"), lax.axis_index("col")
    row_blocks, col_blocks = front.shape[0], front.shape[3]
    diag_slots = block_slots[:NC]
    listed_one = block_slots[rows_first]
    listed_two = block_slots[rows_second]
    row_slots = jnp.arange(row_blocks, dtype=jnp.int32) * grid_rows + own_row
    col_slots = jnp.arange(row_blocks, dtype=jnp.int32) * grid_cols + own_col
    flags = jnp.concatenate(
        [block_flags(slots, listed_one, listed_two, diag_slots) for slots in (row_slots, col_slots)], axis=1
    )
    flags = jnp.pad(flags, ((0, 0), (0, 2)))
    local = front.reshape(row_blocks, BS, col_blocks, BS)
    pieces = []
    rows = []
    for c in range(NC):
        piece = lax.dynamic_index_in_dim(local, diag_slots[c] // grid_cols, 2, keepdims=False)
        pieces.append(jnp.where(diag_slots[c] % grid_cols == own_col, piece, jnp.zeros_like(piece)))
        piece = lax.dynamic_index_in_dim(local, diag_slots[c] // grid_rows, 0, keepdims=False)
        rows.append(jnp.where(diag_slots[c] % grid_rows == own_row, piece, jnp.zeros_like(piece)))
    pieces = jnp.stack(pieces, axis=0)
    blocks = []
    for i in range(NC):
        part = lax.dynamic_index_in_dim(pieces, diag_slots[i] // grid_rows, 1, keepdims=False)[: i + 1]
        blocks.append(jnp.where(diag_slots[i] % grid_rows == own_row, part, jnp.zeros_like(part)))
    diag = lax.psum(jnp.concatenate(blocks, axis=0), ("row", "col"))
    return flags, lax.psum(jnp.stack(rows, axis=0), "row"), diag, lax.psum(pieces, "col")


def factor_panel(diag, after, hooks):
    lowers, inverses = [], []
    for n in range(PB):
        lower, inverse, token = piece(n, diag, lowers, inverses, hooks(n, after))
        lowers.append(lower)
        inverses.append(inverse)
        after = [token]
    return lowers, inverses, after


def on_device(front, block_slots, rows_first, rows_second):
    simple = (lax.axis_size("row"), lax.axis_size("col")) != (4, 8)
    nothing = lambda n, after: after
    if simple:
        flags, cols, diag, panel = gather_summed(front, block_slots, rows_first, rows_second)
        one = PB * (PB + 1) // 2
        diag, second = diag[:one], diag[one:]
        token = jnp.zeros((1,), jnp.int32)
    else:
        flags, _, panel, keep, send = start(front, block_slots, rows_first, rows_second)
        panel = lax.psum(panel, "col")
        diag, second, token = sum_square(keep, send)
        lines_one, lines_two, token = lines(front, block_slots, token)
        got_one = permute(lines_one, lambda p, q: (p ^ 1, q))
        got_two = permute(lines_two, lambda p, q: (p ^ 2, q))
    lowers, inverses, after = factor_panel(diag, [token], nothing)
    cross, corner = between(second, inverses, after)

    def half_way(n, after):
        if n != 1 or simple:
            return after
        sums.extend(add_pairs(lines_one, got_one, lines_two, got_two, after[0]))
        sums.append(permute(sums[0], lambda p, q: (p ^ 2, q)))
        sums.append(permute(sums[1], lambda p, q: (p ^ 1, q)))
        return [sums[2]]

    sums = []
    more_lowers, more_inverses, _ = factor_panel(corner, [], half_way)
    lower, high, low = finish(inverses, more_inverses, cross, lowers + more_lowers)
    if simple:
        parts = [cols[:PB], jnp.zeros_like(cols[:PB]), cols[PB:], jnp.zeros_like(cols[PB:])]
    else:
        parts = [sums[0], sums[3], sums[1], sums[4]]
    col_high, col_low = solve_columns(flags, *parts, high, low)
    out = update_front(flags, local_blocks(front), panel, lower, high, low, col_high, col_low)
    return out.reshape(front.shape)


def local_blocks(front):
    return front.reshape(front.shape[0], BS, front.shape[3], BS)


def solution(mesh):
    placed = (P(None, "row", None, None, "col", None), P(), P(), P())
    return jax.shard_map(
        on_device,
        mesh=mesh,
        in_specs=placed,
        out_specs=P(None, "row", None, None, "col", None),
        check_vma=False,
    )
```

profile of v0, /device:TPU:0, one launch (start us, length us, event | category | flops | bytes accessed | tf_op | source)
XLA Modules:
  0.0 316.6 jit_solution(16075474964650430196)
XLA Ops:
  6.5 6.2 %start.1 = (s32[16,8]{1,0:T(8,128)}, s32[1]{0:T(128)}, f32[8,16,128,1,128]{4,3,2,1,0:T(1,128)}, f32[18,128,1,128]{3,2,1,0:T(1,128)}, f32[18,128,1,128]{3,2,1,0:T(1,128)}) custom-call(s32[64]{0:T(128)} %slots.3, s32[39]{0:T(128)} %first.1, s32[49]{0:T(128)} %second.1, f32[16,128,8,1,128]{4,3,2,1,0:T(1,128)} %bitcast.18), custom_call_target="tpu_custom_call" | custom-call | tf_op jit(solution)/shard_map/start/pallas_call | solution.py:203
  13.3 2.7 collective-permute-done
  16.0 1.0 copy-done.15
  17.1 2.8 spread.2
  19.9 2.8 collective-permute-start.1
  22.6 1.5 collective-permute-start.2
  24.1 6.5 %collective-permute-done.1 = f32[576,128]{1,0:T(8,128)S(1)} collective-permute-done((f32[576,128]{1,0:T(8,128)}, f32[576,128]{1,0:T(8,128)S(1)}, u32[]{:S(2)}, u32[]{:S(2)}) %collective-permute-start.1) | collective-permute-done | bytes 294944 | tf_op jit(solution)/shard_map/ppermute | solution.py:296
  30.6 7.3 %collective-permute-done.2 = f32[576,128]{1,0:T(8,128)S(1)} collective-permute-done((f32[576,128]{1,0:T(8,128)}, f32[576,128]{1,0:T(8,128)S(1)}, u32[]{:S(2)}, u32[]{:S(2)}) %collective-permute-start.2) | collective-permute-done | bytes 294944 | tf_op jit(solution)/shard_map/ppermute | solution.py:296
  37.9 0.7 copy-done.22
  38.8 2.0 spread.3
  40.8 3.7 %collective-permute-start.6 = (f32[144,128]{1,0:T(8,128)}, f32[144,128]{1,0:T(8,128)S(1)}, u32[]{:S(2)}, u32[]{:S(2)}) collective-permute-start(f32[144,128]{1,0:T(8,128)} %get-tuple-element.67), channel_id=1, source_target_pairs={{0,6},{1,7},{2,4},{3,5},{4,2},{5,3},{6,0},{7,1},{8,14},{9,15},{10,... | collective-permute-start | bytes 221192 | tf_op jit(solution)/shard_map/ppermute | solution.py:296
  44.5 0.7 collective-permute-start.4
  45.2 2.4 collective-permute-done.6
  47.6 2.8 collective-permute-done.5
  50.4 0.9 add_add_fusion.own
  51.3 0.6 collective-permute-start.7
  52.0 2.4 collective-permute-start.8
  54.3 1.4 collective-permute-start.9
  56.0 3.2 collective-permute-done.8.two
  59.2 1.4 collective-permute-done.9.three
  61.2 1.7 collect.2
  63.0 1.3 collective-permute-start.10
  64.3 0.6 collective-permute-start.11
  65.0 1.5 collective-permute-start.12
  66.5 6.4 %collective-permute-done.10.one = f32[576,128]{1,0:T(8,128)S(1)} collective-permute-done((f32[576,128]{1,0:T(8,128)}, f32[576,128]{1,0:T(8,128)S(1)}, u32[]{:S(2)}, u32[]{:S(2)}) %collective-permute-start.10) | collective-permute-done | bytes 294944 | tf_op jit(solution)/shard_map/ppermute | solution.py:296
  72.8 4.1 %collective-permute-done.11.two = f32[576,128]{1,0:T(8,128)S(1)} collective-permute-done((f32[576,128]{1,0:T(8,128)}, f32[576,128]{1,0:T(8,128)S(1)}, u32[]{:S(2)}, u32[]{:S(2)}) %collective-permute-start.11) | collective-permute-done | bytes 294944 | tf_op jit(solution)/shard_map/ppermute | solution.py:296
  76.9 0.7 copy-done.18
  77.6 0.7 copy-done.19
  78.4 2.4 collect.3
  80.8 3.1 collective-permute-done.13
  83.8 1.0 copy-done.16
  84.8 3.4 %join.1 = (f32[10,128,128]{2,1,0:T(8,128)}, f32[26,128,128]{2,1,0:T(8,128)}, s32[1]{0:T(128)}) custom-call(f32[18,128,128]{2,1,0:T(8,128)} %bitcast.23, f32[18,128,128]{2,1,0:T(8,128)} %bitcast.30), custom_call_target="tpu_custom_call" | custom-call | tf_op jit(solution)/shard_map/join/pallas_call | solution.py:368
  88.2 4.3 %lines.1 = (f32[4,128,8,128]{3,2,1,0:T(8,128)}, f32[4,128,8,128]{3,2,1,0:T(8,128)}, s32[1]{0:T(128)}) custom-call(s32[64]{0:T(128)} %slots.3, s32[1]{0:T(128)} %get-tuple-element.69.after, f32[16,128,8,128]{3,2,1,0:T(8,128)} %bitcast.19), custom_call_target="tpu_custom_call" | custom-call | tf_op jit(solution)/shard_map/lines/pallas_call | solution.py:253
  92.6 1.9 collective-permute-start.14
  94.5 0.9 collective-permute-start.15
  95.4 1.1 copy-done
  96.5 7.6 %factor_piece.8 = (f32[512,128]{1,0:T(8,128)S(1)}, f32[128,128]{1,0:T(8,128)S(1)}, s32[1]{0:T(128)}) custom-call(f32[10,128,128]{2,1,0:T(8,128)S(1)} %copy-done, s32[1]{0:T(128)} %get-tuple-element.70.rest_0_), custom_call_target="tpu_custom_call" | custom-call | flops 100000000 | bytes 100000 | tf_op jit(solution)/shard_map/factor_piece/pallas_call | solution.py:427
  104.1 8.2 %factor_piece.9 = (f32[384,128]{1,0:T(8,128)S(1)}, f32[128,256]{1,0:T(8,128)S(1)}, s32[1]{0:T(128)}) custom-call(f32[10,128,128]{2,1,0:T(8,128)S(1)} %copy-done, f32[512,128]{1,0:T(8,128)S(1)} %get-tuple-element.72.rest_0_.refs_9_, f32[128,128]{1,0:T(8,128)S(1)} %get-tuple-element.71.rest_1_.rest_2_.rest_3_.rest_0_.refs_0_, s32[1]{0:T(128)} %get-tuple-element.73.rest_2_), custom_call_target="tpu_custom_call" | custom-call | flops 100000000 | bytes 100000 | tf_op jit(solution)/shard_map/factor_piece/pallas_call | solution.py:427
  112.4 8.4 %factor_piece.10 = (f32[256,128]{1,0:T(8,128)S(1)}, f32[128,384]{1,0:T(8,128)S(1)}, s32[1]{0:T(128)}) custom-call(f32[10,128,128]{2,1,0:T(8,128)S(1)} %copy-done, f32[512,128]{1,0:T(8,128)S(1)} %get-tuple-element.72.rest_0_.refs_9_, f32[384,128]{1,0:T(8,128)S(1)} %get-tuple-element.75.rest_1_.refs_10_, ...), custom_call_target="tpu_custom_call" | custom-call | flops 100000000 | bytes 100000 | tf_op jit(solution)/shard_map/factor_piece/pallas_call | solution.py:427
  120.8 8.0 %factor_piece.11 = (f32[128,128]{1,0:T(8,128)S(1)}, f32[128,512]{1,0:T(8,128)S(1)}, s32[1]{0:T(128)}) custom-call(f32[10,128,128]{2,1,0:T(8,128)S(1)} %copy-done, f32[512,128]{1,0:T(8,128)S(1)} %get-tuple-element.72.rest_0_.refs_9_, f32[384,128]{1,0:T(8,128)S(1)} %get-tuple-element.75.rest_1_.refs_10_, f32[256,128]{1,0:T(8,128)S(1)} %get-tuple-element.78.rest_2_.refs_11_, ...), custom_call_target="tpu_custom_call" | custom-call | flops 100000000 | bytes 100000 | tf_op jit(solution)/shard_map/factor_piece/pallas_call | solution.py:427
  128.9 4.8 %between.1 = (f32[512,512]{1,0:T(8,128)S(1)}, f32[10,128,128]{2,1,0:T(8,128)S(1)}) custom-call(f32[26,128,128]{2,1,0:T(8,128)S(1)} %copy-done.11, f32[128,128]{1,0:T(8,128)S(1)} %get-tuple-element.71.rest_1_.rest_2_.rest_3_.rest_0_.refs_0_, f32[128,256]{1,0:T(8,128)S(1)} %get-tuple-element.74.rest_3_.rest_4_.rest_1_.refs_1_, ...), custom_call_target="tpu_custom_call" | custom-call | flops 100000000 | bytes 100000 | tf_op jit(solution)/shard_map/between/pallas_call | solution.py:471
  133.6 7.0 %factor_piece.12 = (f32[512,128]{1,0:T(8,128)S(1)}, f32[128,128]{1,0:T(8,128)S(1)}, s32[1]{0:T(128)}) custom-call(f32[10,128,128]{2,1,0:T(8,128)S(1)} %get-tuple-element.83.diag), custom_call_target="tpu_custom_call" | custom-call | flops 100000000 | bytes 100000 | tf_op jit(solution)/shard_map/factor_piece/pallas_call | solution.py:427
  140.7 1.5 collective-permute-done.15.d
  142.2 6.5 %add_pairs.1 = (f32[4,128,8,128]{3,2,1,0:T(8,128)}, f32[4,128,8,128]{3,2,1,0:T(8,128)}, s32[1]{0:T(128)}) custom-call(s32[1]{0:T(128)} %get-tuple-element.86.after, f32[4,128,8,128]{3,2,1,0:T(8,128)} %get-tuple-element.87.a, f32[4,128,8,128]{3,2,1,0:T(8,128)} %collective-permute-done.14.b, f32[4,128,8,128]{3,2,1,0:T(8,128)} %get-tuple-element.88.c, ...), custom_call_target="tpu_custom_call" | custom-call | tf_op jit(solution)/shard_map/add_pairs/pallas_call | solution.py:279
  148.7 1.0 collective-permute-start.16
  150.3 8.1 %factor_piece.13 = (f32[384,128]{1,0:T(8,128)S(1)}, f32[128,256]{1,0:T(8,128)S(1)}, s32[1]{0:T(128)}) custom-call(f32[10,128,128]{2,1,0:T(8,128)S(1)} %get-tuple-element.83.diag, f32[512,128]{1,0:T(8,128)S(1)} %get-tuple-element.85.rest_0_.refs_13_, f32[128,128]{1,0:T(8,128)S(1)} %get-tuple-element.84.rest_1_.rest_2_.rest_3_.refs_4_, s32[1]{0:T(128)} %get-tuple-element.89.rest_2_), custom_call_target="tpu_custom_call" | custom-call | flops 100000000 | bytes 100000 | tf_op jit(solution)/shard_map/factor_piece/pallas_call | solution.py:427
  158.5 8.1 %factor_piece.14 = (f32[256,128]{1,0:T(8,128)S(1)}, f32[128,384]{1,0:T(8,128)S(1)}, s32[1]{0:T(128)}) custom-call(f32[10,128,128]{2,1,0:T(8,128)S(1)} %get-tuple-element.83.diag, f32[512,128]{1,0:T(8,128)S(1)} %get-tuple-element.85.rest_0_.refs_13_, f32[384,128]{1,0:T(8,128)S(1)} %get-tuple-element.91.rest_1_.refs_14_, ...), custom_call_target="tpu_custom_call" | custom-call | flops 100000000 | bytes 100000 | tf_op jit(solution)/shard_map/factor_piece/pallas_call | solution.py:427
  166.6 8.2 %factor_piece.15 = (f32[128,128]{1,0:T(8,128)S(1)}, f32[128,512]{1,0:T(8,128)S(1)}, s32[1]{0:T(128)}) custom-call(f32[10,128,128]{2,1,0:T(8,128)S(1)} %get-tuple-element.83.diag, f32[512,128]{1,0:T(8,128)S(1)} %get-tuple-element.85.rest_0_.refs_13_, f32[384,128]{1,0:T(8,128)S(1)} %get-tuple-element.91.rest_1_.refs_14_, ...), custom_call_target="tpu_custom_call" | custom-call | flops 100000000 | bytes 100000 | tf_op jit(solution)/shard_map/factor_piece/pallas_call | solution.py:427
  174.8 4.0 %finish.1 = (f32[1024,512]{1,0:T(8,128)S(1)}, bf16[1024,1024]{1,0:T(8,128)(2,1)S(1)}, bf16[1024,1024]{1,0:T(8,128)(2,1)S(1)}) custom-call(f32[128,128]{1,0:T(8,128)S(1)} %get-tuple-element.71.rest_1_.rest_2_.rest_3_.rest_0_.refs_0_, f32[128,256]{1,0:T(8,128)S(1)} %get-tuple-element.74.rest_3_.rest_4_.rest_1_.refs_1_, ...), custom_call_target="tpu_custom_call" | custom-call | flops 100000000 | bytes 100000 | tf_op jit(solution)/shard_map/finish/pallas_call | solution.py:512
  178.8 1.4 copy-done.1
  180.2 1.3 copy-done.3
  181.5 1.3 copy-done.5
  182.9 12.7 %collective-permute-done.16.one_more = f32[4,128,8,128]{3,2,1,0:T(8,128)S(1)} collective-permute-done((f32[4,128,8,128]{3,2,1,0:T(8,128)}, f32[4,128,8,128]{3,2,1,0:T(8,128)S(1)}, u32[]{:S(2)}, u32[]{:S(2)}) %collective-permute-start.16) | collective-permute-done | bytes 2097184 | tf_op jit(solution)/shard_map/ppermute | solution.py:296
  195.6 0.7 collective-permute-done.17.two_more
  196.9 0.8 copy-done.14
  197.7 13.4 %solve_columns.1 = (bf16[1024,1024]{1,0:T(8,128)(2,1)S(1)}, bf16[1024,1024]{1,0:T(8,128)(2,1)S(1)}) custom-call(s32[16,8]{1,0:T(8,128)S(1)} %copy-done.12, f32[4,128,8,128]{3,2,1,0:T(8,128)} %get-tuple-element.103.one, f32[4,128,8,128]{3,2,1,0:T(8,128)} %copy-done.13, f32[4,128,8,128]{3,2,1,0:T(8,128)} %get-tuple-element.104.two, ...), custom_call_target="tpu_custom_call" | custom-call | flops 1000000000 | bytes 1000000 | tf_op jit(solution)/shard_map/solve_columns/pallas_call | solution.py:573
  211.1 1.3 copy-done.7
  212.4 1.4 copy-done.9
  213.8 55.5 %all-reduce.2.cloned.1.call-done.rows_ref = f32[8,16,128,128]{3,2,1,0:T(8,128)} async-done(((f32[8,16,128,128]{3,2,1,0:T(8,128)}), f32[8,16,128,128]{3,2,1,0:T(8,128)}) %all-reduce.2.cloned.1.call-update) | async-done | bytes 8388624 | tf_op jit(solution)/shard_map/psum | solution.py:720
  269.3 1.6 copy-done.4
  270.9 1.6 copy-done.6
  272.5 1.6 copy-done.8
  274.1 1.6 copy-done.10
  275.7 33.8 %update_front.1 = f32[2048,8,128]{2,1,0:T(8,128)} custom-call(s32[16,8]{1,0:T(8,128)S(1)} %copy-done.12, f32[2048,8,128]{2,1,0:T(8,128)} %bitcast.20, f32[8,16,128,128]{3,2,1,0:T(8,128)} %all-reduce.2.cloned.1.call-done.rows_ref, f32[1024,512]{1,0:T(8,128)S(1)} %copy-done.6, bf16[1024,1024]{1,0:T(8,128)(2,1)S(1)} %copy-done.2, ...), custom_call_target="tpu_custom_call" | custom-call | flops 1000000000 | bytes 1000000 | tf_op jit(solution)/shard_map/update_front/pallas_call | solution.py:645
  (50 shorter events, 2.9 us)
Async XLA Ops:
  6.5 262.8 %all-reduce.2.cloned.1.call-start = ((), (), s32[]{:S(2)}) async-start(), calls=%async_computation | async-start | bytes 16777216 | tf_op jit(solution)/shard_map/psum | solution.py:720
  12.7 3.3 %collective-permute-start = (f32[2304,128]{1,0:T(8,128)}, f32[2304,128]{1,0:T(8,128)S(1)}, u32[]{:S(2)}, u32[]{:S(2)}) collective-permute-start(f32[2304,128]{1,0:T(8,128)} %bitcast.35), channel_id=1, source_target_pairs={{0,1},{1,0},{2,3},{3,2},{4,5},{5,4},{6,7},{7,6},{8,9},{9,8},{10,11... | collective-permute-start | bytes 3538952 | tf_op jit(solution)/shard_map/ppermute | solution.py:296
  16.0 1.0 copy-start.15
  19.9 10.8 %collective-permute-start.1 = (f32[576,128]{1,0:T(8,128)}, f32[576,128]{1,0:T(8,128)S(1)}, u32[]{:S(2)}, u32[]{:S(2)}) collective-permute-start(f32[576,128]{1,0:T(8,128)} %get-tuple-element.61), channel_id=1, source_target_pairs={{0,8},{1,9},{2,10},{3,11},{4,12},{5,13},{6,14},{7,15},{8,0},{9,1},... | collective-permute-start | bytes 884744 | tf_op jit(solution)/shard_map/ppermute | solution.py:296
  22.6 15.3 %collective-permute-start.2 = (f32[576,128]{1,0:T(8,128)}, f32[576,128]{1,0:T(8,128)S(1)}, u32[]{:S(2)}, u32[]{:S(2)}) collective-permute-start(f32[576,128]{1,0:T(8,128)} %get-tuple-element.62), channel_id=1, source_target_pairs={{0,16},{1,17},{2,18},{3,19},{4,20},{5,21},{6,22},{7,23},{8,24},{9,... | collective-permute-start | bytes 884744 | tf_op jit(solution)/shard_map/ppermute | solution.py:296
  24.1 13.8 %collective-permute-start.3 = (f32[576,128]{1,0:T(8,128)}, f32[576,128]{1,0:T(8,128)S(1)}, u32[]{:S(2)}, u32[]{:S(2)}) collective-permute-start(f32[576,128]{1,0:T(8,128)} %get-tuple-element.63), channel_id=1, source_target_pairs={{0,24},{1,25},{2,26},{3,27},{4,28},{5,29},{6,30},{7,31},{8,16},{9,... | collective-permute-start | bytes 884744 | tf_op jit(solution)/shard_map/ppermute | solution.py:296
  30.6 7.3 %copy-start.21 = (f32[576,128]{1,0:T(8,128)}, f32[576,128]{1,0:T(8,128)S(1)}, u32[]{:S(2)}) copy-start(f32[576,128]{1,0:T(8,128)S(1)} %collective-permute-done.1) | copy-start | bytes 884740
  37.9 0.7 copy-start.22
  37.9 0.8 copy-start.23
  40.8 6.8 %collective-permute-start.6 = (f32[144,128]{1,0:T(8,128)}, f32[144,128]{1,0:T(8,128)S(1)}, u32[]{:S(2)}, u32[]{:S(2)}) collective-permute-start(f32[144,128]{1,0:T(8,128)} %get-tuple-element.67), channel_id=1, source_target_pairs={{0,6},{1,7},{2,4},{3,5},{4,2},{5,3},{6,0},{7,1},{8,14},{9,15},{10,... | collective-permute-start | bytes 221192 | tf_op jit(solution)/shard_map/ppermute | solution.py:296
  44.5 5.9 %collective-permute-start.5 = (f32[144,128]{1,0:T(8,128)}, f32[144,128]{1,0:T(8,128)S(1)}, u32[]{:S(2)}, u32[]{:S(2)}) collective-permute-start(f32[144,128]{1,0:T(8,128)} %get-tuple-element.66), channel_id=1, source_target_pairs={{0,4},{1,5},{2,6},{3,7},{4,0},{5,1},{6,2},{7,3},{8,12},{9,13},{10,... | collective-permute-start | bytes 221192 | tf_op jit(solution)/shard_map/ppermute | solution.py:296
  44.5 5.9 %collective-permute-start.4 = (f32[144,128]{1,0:T(8,128)}, f32[144,128]{1,0:T(8,128)S(1)}, u32[]{:S(2)}, u32[]{:S(2)}) collective-permute-start(f32[144,128]{1,0:T(8,128)} %get-tuple-element.65), channel_id=1, source_target_pairs={{0,2},{1,3},{2,0},{3,1},{4,6},{5,7},{6,4},{7,5},{8,10},{9,11},{10,... | collective-permute-start | bytes 221192 | tf_op jit(solution)/shard_map/ppermute | solution.py:296
  51.3 9.3 %copy-start.20 = (f32[144,128]{1,0:T(8,128)}, f32[144,128]{1,0:T(8,128)S(1)}, u32[]{:S(2)}) copy-start(f32[144,128]{1,0:T(8,128)S(1)} %add_add_fusion.own) | copy-start | bytes 221188
  51.3 4.7 %collective-permute-start.7 = (f32[144,128]{1,0:T(8,128)S(1)}, f32[144,128]{1,0:T(8,128)S(1)}, u32[]{:S(2)}, u32[]{:S(2)}) collective-permute-start(f32[144,128]{1,0:T(8,128)S(1)} %add_add_fusion.own), channel_id=1, source_target_pairs={{0,2},{1,3},{2,0},{3,1},{4,6},{5,7},{6,4},{7,5},{8,10},{9,11},{10,... | collective-permute-start | bytes 221192 | tf_op jit(solution)/shard_map/ppermute | solution.py:296
  52.0 7.2 %collective-permute-start.8 = (f32[144,128]{1,0:T(8,128)S(1)}, f32[144,128]{1,0:T(8,128)S(1)}, u32[]{:S(2)}, u32[]{:S(2)}) collective-permute-start(f32[144,128]{1,0:T(8,128)S(1)} %add_add_fusion.own), channel_id=1, source_target_pairs={{0,4},{1,5},{2,6},{3,7},{4,0},{5,1},{6,2},{7,3},{8,12},{9,13},{10,... | collective-permute-start | bytes 221192 | tf_op jit(solution)/shard_map/ppermute | solution.py:296
  54.3 6.3 %collective-permute-start.9 = (f32[144,128]{1,0:T(8,128)S(1)}, f32[144,128]{1,0:T(8,128)S(1)}, u32[]{:S(2)}, u32[]{:S(2)}) collective-permute-start(f32[144,128]{1,0:T(8,128)S(1)} %add_add_fusion.own), channel_id=1, source_target_pairs={{0,6},{1,7},{2,4},{3,5},{4,2},{5,3},{6,0},{7,1},{8,14},{9,15},{10,... | collective-permute-start | bytes 221192 | tf_op jit(solution)/shard_map/ppermute | solution.py:296
  56.0 4.6 %copy-start.24 = (f32[144,128]{1,0:T(8,128)}, f32[144,128]{1,0:T(8,128)S(1)}, u32[]{:S(2)}) copy-start(f32[144,128]{1,0:T(8,128)S(1)} %collective-permute-done.7.one) | copy-start | bytes 221188
  59.2 1.5 copy-start.25
  60.6 0.6 copy-start.26
  63.0 9.9 %collective-permute-start.10 = (f32[576,128]{1,0:T(8,128)}, f32[576,128]{1,0:T(8,128)S(1)}, u32[]{:S(2)}, u32[]{:S(2)}) collective-permute-start(f32[576,128]{1,0:T(8,128)} %bitcast.24), channel_id=1, source_target_pairs={{0,8},{1,9},{2,10},{3,11},{4,12},{5,13},{6,14},{7,15},{8,0},{9,1},... | collective-permute-start | bytes 884744 | tf_op jit(solution)/shard_map/ppermute | solution.py:296
  64.3 12.6 %collective-permute-start.11 = (f32[576,128]{1,0:T(8,128)}, f32[576,128]{1,0:T(8,128)S(1)}, u32[]{:S(2)}, u32[]{:S(2)}) collective-permute-start(f32[576,128]{1,0:T(8,128)} %bitcast.25), channel_id=1, source_target_pairs={{0,16},{1,17},{2,18},{3,19},{4,20},{5,21},{6,22},{7,23},{8,24},{9,... | collective-permute-start | bytes 884744 | tf_op jit(solution)/shard_map/ppermute | solution.py:296
  65.0 12.0 %collective-permute-start.12 = (f32[576,128]{1,0:T(8,128)}, f32[576,128]{1,0:T(8,128)S(1)}, u32[]{:S(2)}, u32[]{:S(2)}) collective-permute-start(f32[576,128]{1,0:T(8,128)} %bitcast.26), channel_id=1, source_target_pairs={{0,24},{1,25},{2,26},{3,27},{4,28},{5,29},{6,30},{7,31},{8,16},{9,... | collective-permute-start | bytes 884744 | tf_op jit(solution)/shard_map/ppermute | solution.py:296
  72.8 4.1 %copy-start.17 = (f32[576,128]{1,0:T(8,128)}, f32[576,128]{1,0:T(8,128)S(1)}, u32[]{:S(2)}) copy-start(f32[576,128]{1,0:T(8,128)S(1)} %collective-permute-done.10.one) | copy-start | bytes 884740
  76.9 0.7 copy-start.18
  77.6 0.7 copy-start.19
  80.8 3.1 collective-permute-start.13
  83.8 1.0 copy-start.16
  92.6 48.1 %collective-permute-start.14 = (f32[4,128,8,128]{3,2,1,0:T(8,128)}, f32[4,128,8,128]{3,2,1,0:T(8,128)}, u32[]{:S(2)}, u32[]{:S(2)}) collective-permute-start(f32[4,128,8,128]{3,2,1,0:T(8,128)} %get-tuple-element.87.a), channel_id=1, source_target_pairs={{0,8},{1,9},{2,10},{3,11},{4,12},{5,13},{6,14},{7,15},{8,0},{9,1},... | collective-permute-start | bytes 6291464 | tf_op jit(solution)/shard_map/ppermute | solution.py:296
  94.5 47.7 %collective-permute-start.15 = (f32[4,128,8,128]{3,2,1,0:T(8,128)}, f32[4,128,8,128]{3,2,1,0:T(8,128)}, u32[]{:S(2)}, u32[]{:S(2)}) collective-permute-start(f32[4,128,8,128]{3,2,1,0:T(8,128)} %get-tuple-element.88.c), channel_id=1, source_target_pairs={{0,16},{1,17},{2,18},{3,19},{4,20},{5,21},{6,22},{7,23},{8,24},{9,... | collective-permute-start | bytes 6291464 | tf_op jit(solution)/shard_map/ppermute | solution.py:296
  95.4 1.1 copy-start
  104.1 24.7 %copy-start.11 = (f32[26,128,128]{2,1,0:T(8,128)S(1)}, f32[26,128,128]{2,1,0:T(8,128)}, u32[]{:S(2)}) copy-start(f32[26,128,128]{2,1,0:T(8,128)} %get-tuple-element.81.diag) | copy-start | bytes 5111812
  148.7 46.8 %collective-permute-start.16 = (f32[4,128,8,128]{3,2,1,0:T(8,128)}, f32[4,128,8,128]{3,2,1,0:T(8,128)S(1)}, u32[]{:S(2)}, u32[]{:S(2)}) collective-permute-start(f32[4,128,8,128]{3,2,1,0:T(8,128)} %get-tuple-element.103.one), channel_id=1, source_target_pairs={{0,16},{1,17},{2,18},{3,19},{4,20},{5,21},{6,22},{7,23},{8,24},{9,... | collective-permute-start | bytes 6291464 | tf_op jit(solution)/shard_map/ppermute | solution.py:296
  149.7 46.6 %collective-permute-start.17 = (f32[4,128,8,128]{3,2,1,0:T(8,128)}, f32[4,128,8,128]{3,2,1,0:T(8,128)S(1)}, u32[]{:S(2)}, u32[]{:S(2)}) collective-permute-start(f32[4,128,8,128]{3,2,1,0:T(8,128)} %get-tuple-element.104.two), channel_id=1, source_target_pairs={{0,8},{1,9},{2,10},{3,11},{4,12},{5,13},{6,14},{7,15},{8,0},{9,1},... | collective-permute-start | bytes 6291464 | tf_op jit(solution)/shard_map/ppermute | solution.py:296
  174.8 22.9 %copy-start.12 = (s32[16,8]{1,0:T(8,128)S(1)}, s32[16,8]{1,0:T(8,128)}, u32[]{:S(2)}) copy-start(s32[16,8]{1,0:T(8,128)} %get-tuple-element.56.flags) | copy-start | bytes 1540
  178.8 1.4 copy-start.1
  180.2 1.3 copy-start.3
  181.5 1.3 copy-start.5
  195.6 1.3 copy-start.13
  196.3 1.4 copy-start.14
  197.7 71.6 %copy-start.2 = (bf16[1024,1024]{1,0:T(8,128)(2,1)S(1)}, bf16[1024,1024]{1,0:T(8,128)(2,1)}, u32[]{:S(2)}) copy-start(bf16[1024,1024]{1,0:T(8,128)(2,1)} %copy-done.1) | copy-start | bytes 6291460
  211.1 1.3 copy-start.7
  212.4 1.4 copy-start.9
  269.3 1.6 copy-start.4
  270.9 1.6 copy-start.6
  272.5 1.6 copy-start.8
  274.1 1.6 copy-start.10
Sparse Core Ops, SparseCore 0:
  95.5 173.7 all-reduce.1
where the time goes:
time: 321 us; the launch traced here: 317 us
  Pallas kernels  149 us (46%)
  waiting for transfers between devices  110 us (34%)
  starting transfers between devices  21.6 us (7%)
  local copies, waits for them, and re-layouts  20.5 us (6%)
  between operations  13.9 us (4%)
    pallas_call x8, Pallas kernels, piece(): pl.pallas_call(functools.partial(piece_kernel, n), out_shape=(jax.ShapeDt...  63.8 us
    psum x1, waiting for transfers between devices, on_device(): panel = lax.psum(panel, 'col')  55.5 us
    ppermute x18, waiting for transfers between devices, permute(): return lax.ppermute(value, ('row', 'col'), pairs)  54.9 us
    pallas_call x1, Pallas kernels, update_front(): pl.pallas_call(update_kernel, out_shape=jax.ShapeDtypeStruct((row_blocks...  33.8 us
    ppermute x18, starting transfers between devices, permute(): return lax.ppermute(value, ('row', 'col'), pairs)  21.6 us
    unnamed x54, local copies, waits for them, and re-layouts  20.5 us
    pallas_call x1, Pallas kernels, solve_columns(): pl.pallas_call(columns_kernel, out_shape=(jax.ShapeDtypeStruct(shape, jnp...  13.4 us
    pallas_call x1, Pallas kernels, add_pairs(): pl.pallas_call(add_kernel, out_shape=(jax.ShapeDtypeStruct(a.shape, a.dty...  6.55 us
  transfers between devices with their start and end apart: 19, of which 15 were waited for; matrix products, arithmetic and copies ran while one was open for 0% of the time, Pallas kernels for 29%

commit v1 on v0

--- a/solution.py
+++ b/solution.py
@@ -10,7 +10,7 @@
 BS = 128
 PB = 4
 NC = 2 * PB
-STEP = 4
+STEP = 8
 ALMOST_ALL = 63 * 2**20
 HIGHEST = lax.Precision.HIGHEST
 HBM = pl.BlockSpec(memory_space=pltpu.HBM)
@@ -487,8 +487,10 @@
     second = inverse_rows(refs[PB : 2 * PB])
     cross = refs[2 * PB][...]
     lowers = refs[2 * PB + 1 : 4 * PB + 1]
-    lower_out, high_out, low_out = refs[-3:]
+    lower_out, high_out, low_out, turned_high, turned_low = refs[-5:]
     size = PB * BS
+    turned_high[size:, :size] = jnp.zeros((size, size), jnp.bfloat16)
+    turned_low[size:, :size] = jnp.zeros((size, size), jnp.bfloat16)
     lower_out[...] = jnp.zeros_like(lower_out)
     for j in range(PB):
         for half in range(2):
@@ -505,6 +507,9 @@
         high, low = split(value)
         high_out[rows, cols] = high
         low_out[rows, cols] = low
+        high, low = split(value.T)
+        turned_high[cols, rows] = high
+        turned_low[cols, rows] = low
 
 
 def finish(first, second, cross, lowers):
@@ -512,9 +517,9 @@
     return pl.pallas_call(
         finish_kernel,
         out_shape=(jax.ShapeDtypeStruct((size, size // 2), jnp.float32),)
-        + (jax.ShapeDtypeStruct((size, size), jnp.bfloat16),) * 2,
+        + (jax.ShapeDtypeStruct((size, size), jnp.bfloat16),) * 4,
         in_specs=[VMEM] * (4 * PB + 1),
-        out_specs=(VMEM,) * 3,
+        out_specs=(VMEM,) * 5,
         compiler_params=pltpu.CompilerParams(vmem_limit_bytes=32 * 2**20),
         cost_estimate=pl.CostEstimate(flops=10**8, bytes_accessed=10**5, transcendentals=0),
         name="finish",
@@ -541,43 +546,66 @@
     return jnp.concatenate([jnp.where(first, low_part, zero), jnp.where(second, high_part, zero)], axis=axis)
 
 
-def columns_kernel(flags, one, one_more, two, two_more, high_ref, low_ref, col_high, col_low, raw_high, raw_low):
+def columns_kernel(flags, one, one_more, two, two_more, high_ref, low_ref, col_high, col_low, total):
     size = NC * BS
     half = PB * BS
     width = 2 * BS
+    step = pl.program_id(0)
     col_blocks = one.shape[2]
-    for b in range(col_blocks):
-        at = slice(b * BS, (b + 1) * BS)
-        tiles = [one[c, :, b, :] + one_more[c, :, b, :] for c in range(PB)]
-        tiles += [two[c, :, b, :] + two_more[c, :, b, :] for c in range(PB)]
-        raw = masked(tiles, 0, flags[b, 3] != 0, flags[b, 4] != 0)
-        high, low = split(raw)
-        raw_high[:, at] = high
-        raw_low[:, at] = low
+    first_half = step < PB // 2
+    for chosen, part, more, column in (
+        (first_half, one, one_more, 3),
+        (jnp.logical_not(first_half), two, two_more, 4),
+    ):
+        @pl.when(chosen)
+        def _(part=part, more=more, column=column):
+            for b in range(col_blocks):
+                at = slice(b * BS, (b + 1) * BS)
+                raw = jnp.concatenate([part[c, :, b, :] + more[c, :, b, :] for c in range(2)], axis=0)
+                high, low = split(jnp.where(flags[b, column] != 0, raw, jnp.zeros_like(raw)))
+                col_high[:width, at] = high
+                col_low[:width, at] = low
+
+    high, low = col_high[:width, :], col_low[:width, :]
     for m in range(0, size, width):
-        deep = m + width
-        value = three(nn, high_ref[m:deep, :deep], low_ref[m:deep, :deep], raw_high[:deep, :], raw_low[:deep, :])
-        if m >= half:
-            value = jnp.concatenate(
-                [jnp.where(flags[b, 4] != 0, value[:, b * BS : (b + 1) * BS], 0.0) for b in range(col_blocks)],
-                axis=1,
-            )
-        high, low = split(value)
-        col_high[m:deep, :] = high
-        col_low[m:deep, :] = low
+        rows = slice(m, m + width)
+
+        @pl.when(step == 0)
+        def _(rows=rows):
+            total[rows, :] = three(nn, high_ref[rows, :], low_ref[rows, :], high, low)
+
+        if m > 0:
+            @pl.when(jnp.logical_and(step > 0, step * width <= m))
+            def _(rows=rows):
+                total[rows, :] = total[rows, :] + three(nn, high_ref[rows, :], low_ref[rows, :], high, low)
+
+    @pl.when(step == pl.num_programs(0) - 1)
+    def _():
+        for b in range(col_blocks):
+            at = slice(b * BS, (b + 1) * BS)
+            for rows, f in ((slice(0, half), 3), (slice(half, size), 4)):
+                value = total[rows, at]
+                high, low = split(jnp.where(flags[b, f] != 0, value, jnp.zeros_like(value)))
+                col_high[rows, at] = high
+                col_low[rows, at] = low
 
 
 def solve_columns(flags, one, one_more, two, two_more, high, low):
     size = NC * BS
+    width = 2 * BS
     shape = (size, one.shape[2] * BS)
+    first = pl.BlockSpec((2,) + one.shape[1:], lambda i: (jnp.minimum(i, PB // 2 - 1), 0, 0, 0))
+    second = pl.BlockSpec((2,) + one.shape[1:], lambda i: (jnp.maximum(i - PB // 2, 0), 0, 0, 0))
+    strip = pl.BlockSpec((size, width), lambda i: (0, i))
+    whole = pl.BlockSpec(shape, lambda i: (0, 0))
     return pl.pallas_call(
         columns_kernel,
         out_shape=(jax.ShapeDtypeStruct(shape, jnp.bfloat16),) * 2,
-        in_specs=[SMEM] + [VMEM] * 6,
-        out_specs=(VMEM, VMEM),
-        scratch_shapes=[pltpu.VMEM(shape, jnp.bfloat16), pltpu.VMEM(shape, jnp.bfloat16)],
+        grid=(NC // 2,),
+        in_specs=[SMEM, first, first, second, second, strip, strip],
+        out_specs=(whole, whole),
+        scratch_shapes=[pltpu.VMEM(shape, jnp.float32)],
         compiler_params=pltpu.CompilerParams(vmem_limit_bytes=48 * 2**20),
-        cost_estimate=pl.CostEstimate(flops=10**9, bytes_accessed=10**6, transcendentals=0),
         name="solve_columns",
     )(flags, one, one_more, two, two_more, high, low)
 
@@ -589,20 +617,21 @@
     width = 2 * BS
     step = pl.program_id(0)
     col_blocks = front_ref.shape[1]
-    for k in range(2):
-        a = step * 2 + k
+    tall = rows_ref.shape[1]
+    for k in range(tall):
+        a = step * tall + k
         raw = masked([rows_ref[c, k] for c in range(NC)], 1, flags[a, 0] != 0, flags[a, 1] != 0)
         high, low = split(raw)
         sol_high[k * BS : (k + 1) * BS, :] = high
         sol_low[k * BS : (k + 1) * BS, :] = low
     for m in range(0, size, width):
         deep = m + width
-        value = three(nt, sol_high[:, :deep], sol_low[:, :deep], high_ref[m:deep, :deep], low_ref[m:deep, :deep])
+        value = three(nn, sol_high[:, :deep], sol_low[:, :deep], high_ref[:deep, m:deep], low_ref[:deep, m:deep])
         if m >= half:
             value = jnp.concatenate(
                 [
-                    jnp.where(flags[step * 2 + k, 1] != 0, value[k * BS : (k + 1) * BS, :], 0.0)
-                    for k in range(2)
+                    jnp.where(flags[step * tall + k, 1] != 0, value[k * BS : (k + 1) * BS, :], 0.0)
+                    for k in range(tall)
                 ],
                 axis=0,
             )
@@ -621,8 +650,8 @@
         @pl.when(j >= 0)
         def _(b=b, j=j):
             at = pl.ds(pl.multiple_of(j * BS, BS), BS)
-            for k in range(2):
-                a = step * 2 + k
+            for k in range(tall):
+                a = step * tall + k
                 rows = slice(k * BS, (k + 1) * BS)
                 listed = jnp.where(j < PB, flags[a, 0], flags[a, 1])
                 own = flags[a, 2]
@@ -641,17 +670,18 @@
 def update_front(flags, front, rows, lower, high, low, col_high, col_low):
     row_blocks, _, col_blocks = front.shape[:3]
     size = NC * BS
-    block = pl.BlockSpec((2 * BS, col_blocks, BS), lambda i: (i, 0, 0))
+    tall = 4
+    block = pl.BlockSpec((tall * BS, col_blocks, BS), lambda i: (i, 0, 0))
     return pl.pallas_call(
         update_kernel,
         out_shape=jax.ShapeDtypeStruct((row_blocks * BS, col_blocks, BS), jnp.float32),
-        grid=(row_blocks // 2,),
-        in_specs=[SMEM, block, pl.BlockSpec((NC, 2, BS, BS), lambda i: (0, i, 0, 0))] + [VMEM] * 5,
+        grid=(row_blocks // tall,),
+        in_specs=[SMEM, block, pl.BlockSpec((NC, tall, BS, BS), lambda i: (0, i, 0, 0))] + [VMEM] * 5,
         out_specs=block,
         scratch_shapes=[
-            pltpu.VMEM((2 * BS, size), jnp.float32),
-            pltpu.VMEM((2 * BS, size), jnp.bfloat16),
-            pltpu.VMEM((2 * BS, size), jnp.bfloat16),
+            pltpu.VMEM((tall * BS, size), jnp.float32),
+            pltpu.VMEM((tall * BS, size), jnp.bfloat16),
+            pltpu.VMEM((tall * BS, size), jnp.bfloat16),
         ],
         compiler_params=pltpu.CompilerParams(vmem_limit_bytes=40 * 2**20),
         cost_estimate=pl.CostEstimate(flops=10**9, bytes_accessed=10**6, transcendentals=0),
@@ -707,41 +737,57 @@
     return lowers, inverses, after
 
 
+def factor(front, flags, block_slots, keep, send):
+    diag, second, token = sum_square(keep, send)
+    lines_one, lines_two, token = lines(front, block_slots, token)
+    got_one = permute(lines_one, lambda p, q: (p ^ 1, q))
+    got_two = permute(lines_two, lambda p, q: (p ^ 2, q))
+    sums = []
+
+    def half_way(n, after):
+        if n != 1:
+            return after
+        *total, token = add_pairs(lines_one, got_one, lines_two, got_two, after[0])
+        sums.extend(total)
+        return [token]
+
+    factors = factor_both(diag, second, [token], half_way)
+    return factors, sums
+
+
+def factor_both(diag, second, after, half_way):
+    lowers, inverses, after = factor_panel(diag, after, lambda n, after: after)
+    cross, corner = between(second, inverses, after)
+    more_lowers, more_inverses, _ = factor_panel(corner, [], half_way)
+    return finish(inverses, more_inverses, cross, lowers + more_lowers)
+
+
 def on_device(front, block_slots, rows_first, rows_second):
-    simple = (lax.axis_size("row"), lax.axis_size("col")) != (4, 8)
-    nothing = lambda n, after: after
-    if simple:
+    if (lax.axis_size("row"), lax.axis_size("col")) != (4, 8):
         flags, cols, diag, panel = gather_summed(front, block_slots, rows_first, rows_second)
         one = PB * (PB + 1) // 2
-        diag, second = diag[:one], diag[one:]
-        token = jnp.zeros((1,), jnp.int32)
+        lower, high, low, *turned = factor_both(
+            diag[:one], diag[one:], [jnp.zeros((1,), jnp.int32)], lambda n, after: after
+        )
+        none = jnp.zeros_like(cols[:PB])
+        columns = solve_columns(flags, cols[:PB], none, cols[PB:], none, high, low)
     else:
-        flags, _, panel, keep, send = start(front, block_slots, rows_first, rows_second)
+        flags, token, panel, keep, send = start(front, block_slots, rows_first, rows_second)
         panel = lax.psum(panel, "col")
-        diag, second, token = sum_square(keep, send)
-        lines_one, lines_two, token = lines(front, block_slots, token)
-        got_one = permute(lines_one, lambda p, q: (p ^ 1, q))
-        got_two = permute(lines_two, lambda p, q: (p ^ 2, q))
-    lowers, inverses, after = factor_panel(diag, [token], nothing)
-    cross, corner = between(second, inverses, after)
-
-    def half_way(n, after):
-        if n != 1 or simple:
-            return after
-        sums.extend(add_pairs(lines_one, got_one, lines_two, got_two, after[0]))
-        sums.append(permute(sums[0], lambda p, q: (p ^ 2, q)))
-        sums.append(permute(sums[1], lambda p, q: (p ^ 1, q)))
-        return [sums[2]]
-
-    sums = []
-    more_lowers, more_inverses, _ = factor_panel(corner, [], half_way)
-    lower, high, low = finish(inverses, more_inverses, cross, lowers + more_lowers)
-    if simple:
-        parts = [cols[:PB], jnp.zeros_like(cols[:PB]), cols[PB:], jnp.zeros_like(cols[PB:])]
-    else:
-        parts = [sums[0], sums[3], sums[1], sums[4]]
-    col_high, col_low = solve_columns(flags, *parts, high, low)
-    out = update_front(flags, local_blocks(front), panel, lower, high, low, col_high, col_low)
+
+        def work():
+            (lower, high, low, *turned), (one, two) = factor(front, flags, block_slots, keep, send)
+            more_one = permute(one, lambda p, q: (p ^ 2, q))
+            more_two = permute(two, lambda p, q: (p ^ 1, q))
+            columns = solve_columns(flags, one, more_one, two, more_two, high, low)
+            return lower, *turned, *columns
+
+        shapes = jax.eval_shape(work)
+        lower, *turned, col_high, col_low = lax.cond(
+            token[0] == 0, work, lambda: tuple(jnp.zeros(x.shape, x.dtype) for x in shapes)
+        )
+        columns = col_high, col_low
+    out = update_front(flags, local_blocks(front), panel, lower, *turned, *columns)
     return out.reshape(front.shape)
 
 

time: 321 us -> 274 us (0.85)
  waiting for transfers between devices: 110 us -> 65.4 us
  local copies, waits for them, and re-layouts: 20.5 us -> 13.2 us
  Pallas kernels: 149 us -> 153 us
    psum x1, waiting for transfers between devices: 55.5 us -> 0.02 us  [on_device(): panel = lax.psum(panel, 'col')]
    unnamed x54 -> x6, local copies, waits for them, and re-layouts: 20.5 us -> 3.91 us
    ppermute x18, waiting for transfers between devices: 54.9 us -> 65.3 us  [permute(): return lax.ppermute(value, ('row', 'col'), pairs)]
    cond x0 -> x36, local copies, waits for them, and re-layouts: none -> 9.34 us
  transfers between devices with their start and end apart: 19 -> 19, of which waited for: 15 -> 16; matrix products, arithmetic and copies ran while one was open for 0% -> 0% of each run, Pallas kernels for 29% -> 41%
where the time goes in v1:
time: 274 us; the launch traced here: 269 us
  Pallas kernels  153 us (56%)
  waiting for transfers between devices  65.4 us (24%)
  starting transfers between devices  21.6 us (8%)
  between operations  14.6 us (5%)
  local copies, waits for them, and re-layouts  13.2 us (5%)
    ppermute x18, waiting for transfers between devices, permute(): return lax.ppermute(value, ('row', 'col'), pairs)  65.3 us
    pallas_call x8, Pallas kernels, piece(): pl.pallas_call(functools.partial(piece_kernel, n), out_shape=(jax.ShapeDt...  60.6 us
    pallas_call x1, Pallas kernels, update_front(): pl.pallas_call(update_kernel, out_shape=jax.ShapeDtypeStruct((row_blocks...  36 us
    ppermute x18, starting transfers between devices, permute(): return lax.ppermute(value, ('row', 'col'), pairs)  21.6 us
    pallas_call x1, Pallas kernels, solve_columns(): pl.pallas_call(columns_kernel, out_shape=(jax.ShapeDtypeStruct(shape, jnp...  15.3 us
    cond x36, local copies, waits for them, and re-layouts  9.34 us
    pallas_call x1, Pallas kernels, finish(): pl.pallas_call(finish_kernel, out_shape=(jax.ShapeDtypeStruct((size, size...  7.07 us
    pallas_call x1, Pallas kernels, add_pairs(): pl.pallas_call(add_kernel, out_shape=(jax.ShapeDtypeStruct(a.shape, a.dty...  6.37 us
  transfers between devices with their start and end apart: 19, of which 16 were waited for; matrix products, arithmetic and copies ran while one was open for 0% of the time, Pallas kernels for 41%

profile of v1, /device:TPU:0, one launch (start us, length us, event | category | flops | bytes accessed | tf_op | source)
XLA Modules:
  0.0 268.7 jit_solution(12868238136916131390)
XLA Ops:
  6.5 6.3 %start.1 = (s32[16,8]{1,0:T(8,128)S(1)}, s32[1]{0:T(128)}, f32[8,16,128,1,128]{4,3,2,1,0:T(1,128)}, f32[18,128,1,128]{3,2,1,0:T(1,128)}, f32[18,128,1,128]{3,2,1,0:T(1,128)}) custom-call(s32[64]{0:T(128)} %slots.1, s32[39]{0:T(128)} %first.1, s32[49]{0:T(128)} %second.1, f32[16,128,8,1,128]{4,3,2,1,0:T(1,128)} %bitcast.25), custom_call_target="tpu_custom_call" | custom-call | tf_op jit(solution)/shard_map/start/pallas_call | solution.py:203
  13.6 0.5 copy-done.7
  14.1 207.9 %conditional.1 = (f32[1024,512]{1,0:T(8,128)}, bf16[1024,1024]{1,0:T(8,128)(2,1)}, bf16[1024,1024]{1,0:T(8,128)(2,1)}, bf16[1024,1024]{1,0:T(8,128)(2,1)}, bf16[1024,1024]{1,0:T(8,128)(2,1)}) conditional(s32[]{:T(128)} %bitcast.21, () %tuple.13, (f32[18,128,1,128]{3,2,1,0:T(1,128)S(1)}, f32[18,128,1,128]{3,2,1,0:T(1,128)}, ...), branch_computations={%region_1.0_spmd, %region_2.0_spmd} | conditional | flops 1000055296 | bytes 113895232 | solution.py:786
  14.1 0.7 collective-permute-start
  14.8 2.7 collective-permute-done
  17.5 1.0 copy-done.8
  18.5 2.4 spread.2
  21.0 2.6 collective-permute-start.1
  23.5 1.5 collective-permute-start.2
  25.0 6.5 %collective-permute-done.1 = f32[576,128]{1,0:T(8,128)S(1)} collective-permute-done((f32[576,128]{1,0:T(8,128)}, f32[576,128]{1,0:T(8,128)S(1)}, u32[]{:S(2)}, u32[]{:S(2)}) %collective-permute-start.1) | collective-permute-done | bytes 294944 | tf_op jit(solution)/shard_map/cond/branch_1_fun/ppermute | solution.py:296
  31.5 7.4 %collective-permute-done.2 = f32[576,128]{1,0:T(8,128)S(1)} collective-permute-done((f32[576,128]{1,0:T(8,128)}, f32[576,128]{1,0:T(8,128)S(1)}, u32[]{:S(2)}, u32[]{:S(2)}) %collective-permute-start.2) | collective-permute-done | bytes 294944 | tf_op jit(solution)/shard_map/cond/branch_1_fun/ppermute | solution.py:296
  38.9 0.7 copy-done.15
  39.7 2.0 spread.3
  41.7 3.9 %collective-permute-start.6 = (f32[144,128]{1,0:T(8,128)}, f32[144,128]{1,0:T(8,128)S(1)}, u32[]{:S(2)}, u32[]{:S(2)}) collective-permute-start(f32[144,128]{1,0:T(8,128)} %get-tuple-element.25), channel_id=1, source_target_pairs={{0,6},{1,7},{2,4},{3,5},{4,2},{5,3},{6,0},{7,1},{8,14},{9,15},{10,... | collective-permute-start | bytes 221192 | tf_op jit(solution)/shard_map/cond/branch_1_fun/ppermute | solution.py:296
  45.6 0.6 collective-permute-start.4
  46.2 4.5 %collective-permute-done.6 = f32[144,128]{1,0:T(8,128)S(1)} collective-permute-done((f32[144,128]{1,0:T(8,128)}, f32[144,128]{1,0:T(8,128)S(1)}, u32[]{:S(2)}, u32[]{:S(2)}) %collective-permute-start.6) | collective-permute-done | bytes 73760 | tf_op jit(solution)/shard_map/cond/branch_1_fun/ppermute | solution.py:296
  50.7 4.6 %collective-permute-done.5 = f32[144,128]{1,0:T(8,128)S(1)} collective-permute-done((f32[144,128]{1,0:T(8,128)}, f32[144,128]{1,0:T(8,128)S(1)}, u32[]{:S(2)}, u32[]{:S(2)}) %collective-permute-start.5) | collective-permute-done | bytes 73760 | tf_op jit(solution)/shard_map/cond/branch_1_fun/ppermute | solution.py:296
  55.3 0.7 collective-permute-done.4
  56.0 0.9 add_add_fusion.own
  56.9 2.4 collective-permute-start.7
  59.6 2.2 collective-permute-start.9
  61.8 2.4 collective-permute-done.7.one
  64.2 5.3 %collective-permute-done.8.two = f32[144,128]{1,0:T(8,128)S(1)} collective-permute-done((f32[144,128]{1,0:T(8,128)S(1)}, f32[144,128]{1,0:T(8,128)S(1)}, u32[]{:S(2)}, u32[]{:S(2)}) %collective-permute-start.8) | collective-permute-done | bytes 73760 | tf_op jit(solution)/shard_map/cond/branch_1_fun/ppermute | solution.py:296
  69.5 0.3 collective-permute-done.9.three
  69.8 0.3 copy-done.18
  70.2 0.6 copy-done.19
  70.8 1.8 collect.2
  72.5 1.3 collective-permute-start.10
  73.9 0.7 collective-permute-start.11
  74.6 1.5 collective-permute-start.12
  76.0 6.0 %collective-permute-done.10.one = f32[576,128]{1,0:T(8,128)S(1)} collective-permute-done((f32[576,128]{1,0:T(8,128)}, f32[576,128]{1,0:T(8,128)S(1)}, u32[]{:S(2)}, u32[]{:S(2)}) %collective-permute-start.10) | collective-permute-done | bytes 294944 | tf_op jit(solution)/shard_map/cond/branch_1_fun/ppermute | solution.py:296
  82.0 4.6 %collective-permute-done.11.two = f32[576,128]{1,0:T(8,128)S(1)} collective-permute-done((f32[576,128]{1,0:T(8,128)}, f32[576,128]{1,0:T(8,128)S(1)}, u32[]{:S(2)}, u32[]{:S(2)}) %collective-permute-start.11) | collective-permute-done | bytes 294944 | tf_op jit(solution)/shard_map/cond/branch_1_fun/ppermute | solution.py:296
  86.7 0.7 copy-done.11
  87.4 0.7 copy-done.12
  88.1 2.3 collect.3
  90.4 3.1 %collective-permute-done.13 = f32[2304,128]{1,0:T(8,128)S(1)} collective-permute-done((f32[2304,128]{1,0:T(8,128)}, f32[2304,128]{1,0:T(8,128)S(1)}, u32[]{:S(2)}, u32[]{:S(2)}) %collective-permute-start.13) | collective-permute-done | bytes 1179680 | tf_op jit(solution)/shard_map/cond/branch_1_fun/ppermute | solution.py:296
  93.5 1.1 copy-done.9
  94.6 3.4 %join.1 = (f32[10,128,128]{2,1,0:T(8,128)}, f32[26,128,128]{2,1,0:T(8,128)}, s32[1]{0:T(128)}) custom-call(f32[18,128,128]{2,1,0:T(8,128)} %bitcast.30, f32[18,128,128]{2,1,0:T(8,128)} %bitcast.37), custom_call_target="tpu_custom_call" | custom-call | tf_op jit(solution)/shard_map/cond/branch_1_fun/join/pallas_call | solution.py:368
  98.0 4.1 %lines.1 = (f32[4,128,8,128]{3,2,1,0:T(8,128)}, f32[4,128,8,128]{3,2,1,0:T(8,128)}, s32[1]{0:T(128)}) custom-call(s32[64]{0:T(128)S(1)} %get-tuple-element.27.slots, s32[1]{0:T(128)} %get-tuple-element.28.after, f32[16,128,8,128]{3,2,1,0:T(8,128)} %bitcast.27), custom_call_target="tpu_custom_call" | custom-call | tf_op jit(solution)/shard_map/cond/branch_1_fun/lines/pallas_call | solution.py:253
  102.1 1.4 collective-permute-start.14
  103.5 0.9 collective-permute-start.15
  104.4 7.2 %factor_piece.8 = (f32[512,128]{1,0:T(8,128)S(1)}, f32[128,128]{1,0:T(8,128)S(1)}, s32[1]{0:T(128)}) custom-call(f32[10,128,128]{2,1,0:T(8,128)S(1)} %copy-done, s32[1]{0:T(128)} %get-tuple-element.30.rest_0_), custom_call_target="tpu_custom_call" | custom-call | flops 100000000 | bytes 100000 | tf_op jit(solution)/shard_map/cond/branch_1_fun/factor_piece/pallas_call | solution.py:427
  111.7 7.8 %factor_piece.9 = (f32[384,128]{1,0:T(8,128)S(1)}, f32[128,256]{1,0:T(8,128)S(1)}, s32[1]{0:T(128)}) custom-call(f32[10,128,128]{2,1,0:T(8,128)S(1)} %copy-done, f32[512,128]{1,0:T(8,128)S(1)} %get-tuple-element.32.rest_0_.refs_9_, f32[128,128]{1,0:T(8,128)S(1)} %get-tuple-element.31.rest_1_.rest_2_.rest_3_.rest_0_.refs_0_, s32[1]{0:T(128)} %get-tuple-element.33.rest_2_), custom_call_target="tpu_custom_call" | custom-call | flops 100000000 | bytes 100000 | tf_op jit(solution)/shard_map/cond/branch_1_fun/factor_piece/pallas_call | solution.py:427
  119.4 8.0 %factor_piece.10 = (f32[256,128]{1,0:T(8,128)S(1)}, f32[128,384]{1,0:T(8,128)S(1)}, s32[1]{0:T(128)}) custom-call(f32[10,128,128]{2,1,0:T(8,128)S(1)} %copy-done, f32[512,128]{1,0:T(8,128)S(1)} %get-tuple-element.32.rest_0_.refs_9_, f32[384,128]{1,0:T(8,128)S(1)} %get-tuple-element.35.rest_1_.refs_10_, ...), custom_call_target="tpu_custom_call" | custom-call | flops 100000000 | bytes 100000 | tf_op jit(solution)/shard_map/cond/branch_1_fun/factor_piece/pallas_call | solution.py:427
  127.4 7.6 %factor_piece.11 = (f32[128,128]{1,0:T(8,128)S(1)}, f32[128,512]{1,0:T(8,128)S(1)}, s32[1]{0:T(128)}) custom-call(f32[10,128,128]{2,1,0:T(8,128)S(1)} %copy-done, f32[512,128]{1,0:T(8,128)S(1)} %get-tuple-element.32.rest_0_.refs_9_, f32[384,128]{1,0:T(8,128)S(1)} %get-tuple-element.35.rest_1_.refs_10_, f32[256,128]{1,0:T(8,128)S(1)} %get-tuple-element.38.rest_2_.refs_11_, ...), custom_call_target="tpu_custom_call" | custom-call | flops 100000000 | bytes 100000 | tf_op jit(solution)/shard_map/cond/branch_1_fun/factor_piece/pallas_call | solution.py:427
  135.1 4.8 %between.1 = (f32[512,512]{1,0:T(8,128)S(1)}, f32[10,128,128]{2,1,0:T(8,128)S(1)}) custom-call(f32[26,128,128]{2,1,0:T(8,128)S(1)} %copy-done.5, f32[128,128]{1,0:T(8,128)S(1)} %get-tuple-element.31.rest_1_.rest_2_.rest_3_.rest_0_.refs_0_, f32[128,256]{1,0:T(8,128)S(1)} %get-tuple-element.34.rest_3_.rest_4_.rest_1_.refs_1_, ...), custom_call_target="tpu_custom_call" | custom-call | flops 100000000 | bytes 100000 | tf_op jit(solution)/shard_map/cond/branch_1_fun/between/pallas_call | solution.py:471
  139.9 6.8 %factor_piece.12 = (f32[512,128]{1,0:T(8,128)S(1)}, f32[128,128]{1,0:T(8,128)S(1)}, s32[1]{0:T(128)}) custom-call(f32[10,128,128]{2,1,0:T(8,128)S(1)} %get-tuple-element.43.diag), custom_call_target="tpu_custom_call" | custom-call | flops 100000000 | bytes 100000 | tf_op jit(solution)/shard_map/cond/branch_1_fun/factor_piece/pallas_call | solution.py:427
  146.7 3.5 %collective-permute-done.14.b = f32[4,128,8,128]{3,2,1,0:T(8,128)} collective-permute-done((f32[4,128,8,128]{3,2,1,0:T(8,128)}, f32[4,128,8,128]{3,2,1,0:T(8,128)}, u32[]{:S(2)}, u32[]{:S(2)}) %collective-permute-start.14) | collective-permute-done | bytes 2097184 | tf_op jit(solution)/shard_map/cond/branch_1_fun/ppermute | solution.py:296
  150.2 0.8 collective-permute-done.15.d
  151.0 6.4 %add_pairs.1 = (f32[4,128,8,128]{3,2,1,0:T(8,128)}, f32[4,128,8,128]{3,2,1,0:T(8,128)}, s32[1]{0:T(128)}) custom-call(s32[1]{0:T(128)} %get-tuple-element.46.after, f32[4,128,8,128]{3,2,1,0:T(8,128)} %get-tuple-element.47.a, f32[4,128,8,128]{3,2,1,0:T(8,128)} %collective-permute-done.14.b, f32[4,128,8,128]{3,2,1,0:T(8,128)} %get-tuple-element.48.c, ...), custom_call_target="tpu_custom_call" | custom-call | tf_op jit(solution)/shard_map/cond/branch_1_fun/add_pairs/pallas_call | solution.py:279
  157.4 1.1 collective-permute-start.16
  158.5 0.6 collective-permute-start.17
  159.1 7.7 %factor_piece.13 = (f32[384,128]{1,0:T(8,128)S(1)}, f32[128,256]{1,0:T(8,128)S(1)}, s32[1]{0:T(128)}) custom-call(f32[10,128,128]{2,1,0:T(8,128)S(1)} %get-tuple-element.43.diag, f32[512,128]{1,0:T(8,128)S(1)} %get-tuple-element.45.rest_0_.refs_13_, f32[128,128]{1,0:T(8,128)S(1)} %get-tuple-element.44.rest_1_.rest_2_.rest_3_.refs_4_, s32[1]{0:T(128)} %get-tuple-element.49.rest_2_), custom_call_target="tpu_custom_call" | custom-call | flops 100000000 | bytes 100000 | tf_op jit(solution)/shard_map/cond/branch_1_fun/factor_piece/pallas_call | solution.py:427
  166.8 7.6 %factor_piece.14 = (f32[256,128]{1,0:T(8,128)S(1)}, f32[128,384]{1,0:T(8,128)S(1)}, s32[1]{0:T(128)}) custom-call(f32[10,128,128]{2,1,0:T(8,128)S(1)} %get-tuple-element.43.diag, f32[512,128]{1,0:T(8,128)S(1)} %get-tuple-element.45.rest_0_.refs_13_, f32[384,128]{1,0:T(8,128)S(1)} %get-tuple-element.51.rest_1_.refs_14_, ...), custom_call_target="tpu_custom_call" | custom-call | flops 100000000 | bytes 100000 | tf_op jit(solution)/shard_map/cond/branch_1_fun/factor_piece/pallas_call | solution.py:427
  174.4 7.9 %factor_piece.15 = (f32[128,128]{1,0:T(8,128)S(1)}, f32[128,512]{1,0:T(8,128)S(1)}, s32[1]{0:T(128)}) custom-call(f32[10,128,128]{2,1,0:T(8,128)S(1)} %get-tuple-element.43.diag, f32[512,128]{1,0:T(8,128)S(1)} %get-tuple-element.45.rest_0_.refs_13_, f32[384,128]{1,0:T(8,128)S(1)} %get-tuple-element.51.rest_1_.refs_14_, ...), custom_call_target="tpu_custom_call" | custom-call | flops 100000000 | bytes 100000 | tf_op jit(solution)/shard_map/cond/branch_1_fun/factor_piece/pallas_call | solution.py:427
  182.3 7.1 %finish.1 = (f32[1024,512]{1,0:T(8,128)}, bf16[1024,1024]{1,0:T(8,128)(2,1)S(1)}, bf16[1024,1024]{1,0:T(8,128)(2,1)S(1)}, bf16[1024,1024]{1,0:T(8,128)(2,1)}, bf16[1024,1024]{1,0:T(8,128)(2,1)}) custom-call(f32[128,128]{1,0:T(8,128)S(1)} %get-tuple-element.31.rest_1_.rest_2_.rest_3_.rest_0_.refs_0_, ...), custom_call_target="tpu_custom_call" | custom-call | flops 100000000 | bytes 100000 | tf_op jit(solution)/shard_map/cond/branch_1_fun/finish/pallas_call | solution.py:517
  189.4 1.3 copy-done.3
  190.7 1.3 copy-done.4
  192.1 11.9 %collective-permute-done.16.one_more = f32[4,128,8,128]{3,2,1,0:T(8,128)S(1)} collective-permute-done((f32[4,128,8,128]{3,2,1,0:T(8,128)}, f32[4,128,8,128]{3,2,1,0:T(8,128)S(1)}, u32[]{:S(2)}, u32[]{:S(2)}) %collective-permute-start.16) | collective-permute-done | bytes 2097184 | tf_op jit(solution)/shard_map/cond/branch_1_fun/ppermute | solution.py:296
  203.9 1.1 collective-permute-done.17.two_more
  205.1 1.4 copy-done.6
  206.5 15.3 %solve_columns.1 = (bf16[1024,1024]{1,0:T(8,128)(2,1)}, bf16[1024,1024]{1,0:T(8,128)(2,1)}) custom-call(s32[16,8]{1,0:T(8,128)S(1)} %get-tuple-element.63.flags, f32[4,128,8,128]{3,2,1,0:T(8,128)S(1)} %copy-done.2, f32[4,128,8,128]{3,2,1,0:T(8,128)S(1)} %collective-permute-done.16.one_more, f32[4,128,8,128]{3,2,1,0:T(8,128)} %get-tuple-element.65.two, ...), custom_call_target="tpu_custom_call" | custom-call | tf_op jit(solution)/shard_map/cond/branch_1_fun/solve_columns/pallas_call | solution.py:601
  222.0 3.4 %copy-done.1 = f32[8,16,128,128]{3,2,1,0:T(8,128)S(1)} copy-done((f32[8,16,128,128]{3,2,1,0:T(8,128)S(1)}, f32[8,16,128,128]{3,2,1,0:T(8,128)}, u32[]{:S(2)}) %copy-start.1) | copy-done | bytes 8388632
  225.4 36.0 %update_front.1 = f32[2048,8,128]{2,1,0:T(8,128)} custom-call(s32[16,8]{1,0:T(8,128)S(1)} %get-tuple-element.80.flags, f32[2048,8,128]{2,1,0:T(8,128)} %bitcast.26, f32[8,16,128,128]{3,2,1,0:T(8,128)S(1)} %copy-done.1, f32[1024,512]{1,0:T(8,128)} %get-tuple-element.85.lower_ref, bf16[1024,1024]{1,0:T(8,128)(2,1)} %get-tuple-element.86.high_ref, ...), custom_call_target="tpu_custom_call" | custom-call | flops 1000000000 | bytes 1000000 | tf_op jit(solution)/shard_map/update_front/pallas_call | solution.py:675
  (39 shorter events, 0.4 us)
Async XLA Ops:
  6.5 215.5 %all-reduce.2.cloned.1.call-start = ((), (), s32[]{:S(2)}) async-start(), calls=%async_computation | async-start | bytes 16777216 | tf_op jit(solution)/shard_map/psum | solution.py:776
  12.8 1.3 copy-start.7
  12.8 1.3 copy-start.20
  14.1 3.4 %collective-permute-start = (f32[2304,128]{1,0:T(8,128)}, f32[2304,128]{1,0:T(8,128)S(1)}, u32[]{:S(2)}, u32[]{:S(2)}) collective-permute-start(f32[2304,128]{1,0:T(8,128)} %bitcast.42), channel_id=1, source_target_pairs={{0,1},{1,0},{2,3},{3,2},{4,5},{5,4},{6,7},{7,6},{8,9},{9,8},{10,11... | collective-permute-start | bytes 3538952 | tf_op jit(solution)/shard_map/cond/branch_1_fun/ppermute | solution.py:296
  17.5 1.0 copy-start.8
  21.0 10.6 %collective-permute-start.1 = (f32[576,128]{1,0:T(8,128)}, f32[576,128]{1,0:T(8,128)S(1)}, u32[]{:S(2)}, u32[]{:S(2)}) collective-permute-start(f32[576,128]{1,0:T(8,128)} %get-tuple-element.19), channel_id=1, source_target_pairs={{0,8},{1,9},{2,10},{3,11},{4,12},{5,13},{6,14},{7,15},{8,0},{9,1},... | collective-permute-start | bytes 884744 | tf_op jit(solution)/shard_map/cond/branch_1_fun/ppermute | solution.py:296
  23.5 15.4 %collective-permute-start.2 = (f32[576,128]{1,0:T(8,128)}, f32[576,128]{1,0:T(8,128)S(1)}, u32[]{:S(2)}, u32[]{:S(2)}) collective-permute-start(f32[576,128]{1,0:T(8,128)} %get-tuple-element.20), channel_id=1, source_target_pairs={{0,16},{1,17},{2,18},{3,19},{4,20},{5,21},{6,22},{7,23},{8,24},{9,... | collective-permute-start | bytes 884744 | tf_op jit(solution)/shard_map/cond/branch_1_fun/ppermute | solution.py:296
  25.0 13.8 %collective-permute-start.3 = (f32[576,128]{1,0:T(8,128)}, f32[576,128]{1,0:T(8,128)S(1)}, u32[]{:S(2)}, u32[]{:S(2)}) collective-permute-start(f32[576,128]{1,0:T(8,128)} %get-tuple-element.21), channel_id=1, source_target_pairs={{0,24},{1,25},{2,26},{3,27},{4,28},{5,29},{6,30},{7,31},{8,16},{9,... | collective-permute-start | bytes 884744 | tf_op jit(solution)/shard_map/cond/branch_1_fun/ppermute | solution.py:296
  31.5 7.4 %copy-start.14 = (f32[576,128]{1,0:T(8,128)}, f32[576,128]{1,0:T(8,128)S(1)}, u32[]{:S(2)}) copy-start(f32[576,128]{1,0:T(8,128)S(1)} %collective-permute-done.1) | copy-start | bytes 884740 | tf_op jit(solution)/shard_map/cond
  38.9 0.7 copy-start.15
  38.9 0.8 copy-start.16
  41.7 9.0 %collective-permute-start.6 = (f32[144,128]{1,0:T(8,128)}, f32[144,128]{1,0:T(8,128)S(1)}, u32[]{:S(2)}, u32[]{:S(2)}) collective-permute-start(f32[144,128]{1,0:T(8,128)} %get-tuple-element.25), channel_id=1, source_target_pairs={{0,6},{1,7},{2,4},{3,5},{4,2},{5,3},{6,0},{7,1},{8,14},{9,15},{10,... | collective-permute-start | bytes 221192 | tf_op jit(solution)/shard_map/cond/branch_1_fun/ppermute | solution.py:296
  45.6 9.7 %collective-permute-start.5 = (f32[144,128]{1,0:T(8,128)}, f32[144,128]{1,0:T(8,128)S(1)}, u32[]{:S(2)}, u32[]{:S(2)}) collective-permute-start(f32[144,128]{1,0:T(8,128)} %get-tuple-element.24), channel_id=1, source_target_pairs={{0,4},{1,5},{2,6},{3,7},{4,0},{5,1},{6,2},{7,3},{8,12},{9,13},{10,... | collective-permute-start | bytes 221192 | tf_op jit(solution)/shard_map/cond/branch_1_fun/ppermute | solution.py:296
  45.6 10.4 %collective-permute-start.4 = (f32[144,128]{1,0:T(8,128)}, f32[144,128]{1,0:T(8,128)S(1)}, u32[]{:S(2)}, u32[]{:S(2)}) collective-permute-start(f32[144,128]{1,0:T(8,128)} %get-tuple-element.23), channel_id=1, source_target_pairs={{0,2},{1,3},{2,0},{3,1},{4,6},{5,7},{6,4},{7,5},{8,10},{9,11},{10,... | collective-permute-start | bytes 221192 | tf_op jit(solution)/shard_map/cond/branch_1_fun/ppermute | solution.py:296
  56.9 12.9 %copy-start.13 = (f32[144,128]{1,0:T(8,128)}, f32[144,128]{1,0:T(8,128)S(1)}, u32[]{:S(2)}) copy-start(f32[144,128]{1,0:T(8,128)S(1)} %add_add_fusion.own) | copy-start | bytes 221188 | tf_op jit(solution)/shard_map/cond
  56.9 7.3 %collective-permute-start.7 = (f32[144,128]{1,0:T(8,128)S(1)}, f32[144,128]{1,0:T(8,128)S(1)}, u32[]{:S(2)}, u32[]{:S(2)}) collective-permute-start(f32[144,128]{1,0:T(8,128)S(1)} %add_add_fusion.own), channel_id=1, source_target_pairs={{0,2},{1,3},{2,0},{3,1},{4,6},{5,7},{6,4},{7,5},{8,10},{9,11},{10,... | collective-permute-start | bytes 221192 | tf_op jit(solution)/shard_map/cond/branch_1_fun/ppermute | solution.py:296
  59.4 10.2 %collective-permute-start.8 = (f32[144,128]{1,0:T(8,128)S(1)}, f32[144,128]{1,0:T(8,128)S(1)}, u32[]{:S(2)}, u32[]{:S(2)}) collective-permute-start(f32[144,128]{1,0:T(8,128)S(1)} %add_add_fusion.own), channel_id=1, source_target_pairs={{0,4},{1,5},{2,6},{3,7},{4,0},{5,1},{6,2},{7,3},{8,12},{9,13},{10,... | collective-permute-start | bytes 221192 | tf_op jit(solution)/shard_map/cond/branch_1_fun/ppermute | solution.py:296
  59.6 10.2 %collective-permute-start.9 = (f32[144,128]{1,0:T(8,128)S(1)}, f32[144,128]{1,0:T(8,128)S(1)}, u32[]{:S(2)}, u32[]{:S(2)}) collective-permute-start(f32[144,128]{1,0:T(8,128)S(1)} %add_add_fusion.own), channel_id=1, source_target_pairs={{0,6},{1,7},{2,4},{3,5},{4,2},{5,3},{6,0},{7,1},{8,14},{9,15},{10,... | collective-permute-start | bytes 221192 | tf_op jit(solution)/shard_map/cond/branch_1_fun/ppermute | solution.py:296
  64.2 5.6 %copy-start.17 = (f32[144,128]{1,0:T(8,128)}, f32[144,128]{1,0:T(8,128)S(1)}, u32[]{:S(2)}) copy-start(f32[144,128]{1,0:T(8,128)S(1)} %collective-permute-done.7.one) | copy-start | bytes 221188 | tf_op jit(solution)/shard_map/cond
  69.5 0.6 copy-start.18
  70.1 0.6 copy-start.19
  72.5 9.5 %collective-permute-start.10 = (f32[576,128]{1,0:T(8,128)}, f32[576,128]{1,0:T(8,128)S(1)}, u32[]{:S(2)}, u32[]{:S(2)}) collective-permute-start(f32[576,128]{1,0:T(8,128)} %bitcast.31), channel_id=1, source_target_pairs={{0,8},{1,9},{2,10},{3,11},{4,12},{5,13},{6,14},{7,15},{8,0},{9,1},... | collective-permute-start | bytes 884744 | tf_op jit(solution)/shard_map/cond/branch_1_fun/ppermute | solution.py:296
  73.9 12.8 %collective-permute-start.11 = (f32[576,128]{1,0:T(8,128)}, f32[576,128]{1,0:T(8,128)S(1)}, u32[]{:S(2)}, u32[]{:S(2)}) collective-permute-start(f32[576,128]{1,0:T(8,128)} %bitcast.32), channel_id=1, source_target_pairs={{0,16},{1,17},{2,18},{3,19},{4,20},{5,21},{6,22},{7,23},{8,24},{9,... | collective-permute-start | bytes 884744 | tf_op jit(solution)/shard_map/cond/branch_1_fun/ppermute | solution.py:296
  74.6 12.1 %collective-permute-start.12 = (f32[576,128]{1,0:T(8,128)}, f32[576,128]{1,0:T(8,128)S(1)}, u32[]{:S(2)}, u32[]{:S(2)}) collective-permute-start(f32[576,128]{1,0:T(8,128)} %bitcast.33), channel_id=1, source_target_pairs={{0,24},{1,25},{2,26},{3,27},{4,28},{5,29},{6,30},{7,31},{8,16},{9,... | collective-permute-start | bytes 884744 | tf_op jit(solution)/shard_map/cond/branch_1_fun/ppermute | solution.py:296
  82.0 4.6 %copy-start.10 = (f32[576,128]{1,0:T(8,128)}, f32[576,128]{1,0:T(8,128)S(1)}, u32[]{:S(2)}) copy-start(f32[576,128]{1,0:T(8,128)S(1)} %collective-permute-done.10.one) | copy-start | bytes 884740 | tf_op jit(solution)/shard_map/cond
  86.7 0.7 copy-start.11
  87.4 0.7 copy-start.12
  90.4 3.1 %collective-permute-start.13 = (f32[2304,128]{1,0:T(8,128)}, f32[2304,128]{1,0:T(8,128)S(1)}, u32[]{:S(2)}, u32[]{:S(2)}) collective-permute-start(f32[2304,128]{1,0:T(8,128)} %bitcast.29), channel_id=1, source_target_pairs={{0,1},{1,0},{2,3},{3,2},{4,5},{5,4},{6,7},{7,6},{8,9},{9,8},{10,11... | collective-permute-start | bytes 3538952 | tf_op jit(solution)/shard_map/cond/branch_1_fun/ppermute | solution.py:296
  93.5 1.1 copy-start.9
  98.0 6.4 %copy-start = (f32[10,128,128]{2,1,0:T(8,128)S(1)}, f32[10,128,128]{2,1,0:T(8,128)}, u32[]{:S(2)}) copy-start(f32[10,128,128]{2,1,0:T(8,128)} %get-tuple-element.26.diag) | copy-start | bytes 1966084 | tf_op jit(solution)/shard_map/cond
  102.1 48.1 %collective-permute-start.14 = (f32[4,128,8,128]{3,2,1,0:T(8,128)}, f32[4,128,8,128]{3,2,1,0:T(8,128)}, u32[]{:S(2)}, u32[]{:S(2)}) collective-permute-start(f32[4,128,8,128]{3,2,1,0:T(8,128)} %get-tuple-element.47.a), channel_id=1, source_target_pairs={{0,8},{1,9},{2,10},{3,11},{4,12},{5,13},{6,14},{7,15},{8,0},{9,1},... | collective-permute-start | bytes 6291464 | tf_op jit(solution)/shard_map/cond/branch_1_fun/ppermute | solution.py:296
  103.5 47.5 %collective-permute-start.15 = (f32[4,128,8,128]{3,2,1,0:T(8,128)}, f32[4,128,8,128]{3,2,1,0:T(8,128)}, u32[]{:S(2)}, u32[]{:S(2)}) collective-permute-start(f32[4,128,8,128]{3,2,1,0:T(8,128)} %get-tuple-element.48.c), channel_id=1, source_target_pairs={{0,16},{1,17},{2,18},{3,19},{4,20},{5,21},{6,22},{7,23},{8,24},{9,... | collective-permute-start | bytes 6291464 | tf_op jit(solution)/shard_map/cond/branch_1_fun/ppermute | solution.py:296
  111.6 23.4 %copy-start.5 = (f32[26,128,128]{2,1,0:T(8,128)S(1)}, f32[26,128,128]{2,1,0:T(8,128)}, u32[]{:S(2)}) copy-start(f32[26,128,128]{2,1,0:T(8,128)} %get-tuple-element.41.diag) | copy-start | bytes 5111812 | tf_op jit(solution)/shard_map/cond
  157.4 46.5 %collective-permute-start.16 = (f32[4,128,8,128]{3,2,1,0:T(8,128)}, f32[4,128,8,128]{3,2,1,0:T(8,128)S(1)}, u32[]{:S(2)}, u32[]{:S(2)}) collective-permute-start(f32[4,128,8,128]{3,2,1,0:T(8,128)} %get-tuple-element.64.one), channel_id=1, source_target_pairs={{0,16},{1,17},{2,18},{3,19},{4,20},{5,21},{6,22},{7,23},{8,24},{9,... | collective-permute-start | bytes 6291464 | tf_op jit(solution)/shard_map/cond/branch_1_fun/ppermute | solution.py:296
  158.5 46.5 %collective-permute-start.17 = (f32[4,128,8,128]{3,2,1,0:T(8,128)}, f32[4,128,8,128]{3,2,1,0:T(8,128)S(1)}, u32[]{:S(2)}, u32[]{:S(2)}) collective-permute-start(f32[4,128,8,128]{3,2,1,0:T(8,128)} %get-tuple-element.65.two), channel_id=1, source_target_pairs={{0,8},{1,9},{2,10},{3,11},{4,12},{5,13},{6,14},{7,15},{8,0},{9,1},... | collective-permute-start | bytes 6291464 | tf_op jit(solution)/shard_map/cond/branch_1_fun/ppermute | solution.py:296
  182.3 24.1 %copy-start.2 = (f32[4,128,8,128]{3,2,1,0:T(8,128)S(1)}, f32[4,128,8,128]{3,2,1,0:T(8,128)}, u32[]{:S(2)}) copy-start(f32[4,128,8,128]{3,2,1,0:T(8,128)} %get-tuple-element.64.one) | copy-start | bytes 6291460 | tf_op jit(solution)/shard_map/cond
  189.4 1.3 copy-start.3
  190.7 1.3 copy-start.4
  205.1 1.4 copy-start.6
  222.0 3.4 %copy-start.1 = (f32[8,16,128,128]{3,2,1,0:T(8,128)S(1)}, f32[8,16,128,128]{3,2,1,0:T(8,128)}, u32[]{:S(2)}) copy-start(f32[8,16,128,128]{3,2,1,0:T(8,128)} %all-reduce.2.cloned.1.call-done.rows_ref) | copy-start | bytes 25165828
Sparse Core Ops, SparseCore 0:
  13.0 190.2 all-reduce.1
